TPU v7x, 1024 devices: a whole 4x4x32 slice. The times are simulated.
1024 devices in a mesh: dp: 32 (over z), grp: 32 (over x, y, core).
Axes of the slice: x: 4, y: 4, z: 32, core: 2. Of those that a mesh axis runs over, the one named last changes fastest.
Arguments:
- acts: bfloat16 [4096, 16384], P('dp', 'grp')
- grads_out: bfloat16 [4096, 131072], P('dp', 'grp')
- owner_of: int32 [256], replicated, may hold values from 0 to 31, as said below
- factors: float32 [32, 32, 512, 512], P('grp', 'dp'), as said below
Outputs:
- new_factors: float32 [32, 32, 512, 512], P('grp', 'dp')
- preconditioned: bfloat16 [32, 32, 256, 512], P('grp', 'dp')
Inputs may be any that keep to these rules, and one draw needn't show every extreme that they name: `owner_of`: the 8 blocks of one index of grp have distinct owners; each owner holds at most 16 blocks, and some owner holds exactly 16. Every factors[o, d] is symmetric positive definite.
All inputs are finite; a program needn't handle non-finite values.
Results may differ from a plain program's by a relative error of at most 0.04.
Values may be sent and summed in bfloat16 or wider, within the bound.
No kernel may reach another device: no remote copies, remote signals or barrier semaphores. Data moves between devices by JAX's collectives and lax.ppermute only.
A program may use at most 32 MiB of HBM per device.

v0:
```python
import jax
import jax.numpy as jnp
from jax import lax
from jax.sharding import PartitionSpec as P

NEWTON = 2


decay_rate = 0.95


def swapped(block, axis, distance):
    count = lax.axis_size(axis)
    route = []
    for low in range(count):
        high = low | 1 << distance
        if high != low and high < count:
            route += [(low, high), (high, low)]
    return lax.ppermute(block, axis, route)


def inverse_root(statistic):
    highest = lax.Precision.HIGHEST
    norm_value = jnp.sqrt(jnp.sum(statistic * statistic))
    identity = jnp.eye(statistic.shape[0], dtype=jnp.float32)
    current = statistic / norm_value
    start_scale = norm_value ** (-0.25)
    estimate = identity
    for newton_step in range(NEWTON):
        factor = (5.0 * identity - current) * 0.25
        if newton_step == 0:
            estimate = start_scale * factor
        else:
            estimate = jnp.dot(estimate, factor, precision=highest)
        if newton_step + 1 < NEWTON:
            square = jnp.dot(factor, factor, precision=highest)
            fourth = jnp.dot(square, square, precision=highest)
            current = jnp.dot(fourth, current, precision=highest)
    return estimate.astype(jnp.bfloat16)


def per_device(acts, grads_out, owner_of, factors):
    dp_count = lax.axis_size("dp")
    grp_count = lax.axis_size("grp")
    block_width = acts.shape[1]
    slab_rows = block_width // dp_count
    per_group = grads_out.shape[1] // block_width
    dp_where = lax.axis_index("dp")
    grp_where = lax.axis_index("grp")
    summed = lax.psum_scatter(
        lax.dot_general(
            acts, grads_out, (((0,), (0,)), ((), ())), preferred_element_type=jnp.float32
        ).astype(jnp.bfloat16),
        "dp",
        scatter_dimension=0,
        tiled=True,
    )
    grad_rows = summed.reshape(slab_rows, per_group, block_width)
    block_count = owner_of.shape[0]
    block_ids = jnp.arange(block_count, dtype=jnp.int32)
    same_owner = owner_of[:, None] == owner_of[None, :]
    earlier = block_ids[None, :] < block_ids[:, None]
    slot_of = jnp.sum((same_owner & earlier).astype(jnp.int32), axis=1)
    owner_ids = jnp.arange(grp_count, dtype=jnp.int32)
    local_owners = lax.dynamic_slice_in_dim(owner_of, grp_where * per_group, per_group)
    chooser = (owner_ids[:, None] == local_owners[None, :]).astype(jnp.bfloat16)
    outgoing = jnp.einsum(
        "oj,sjc->osc", chooser, grad_rows, preferred_element_type=jnp.float32
    ).astype(jnp.bfloat16)
    incoming = lax.all_to_all(outgoing, "grp", split_axis=0, concat_axis=0, tiled=True)
    held_here = owner_of == grp_where
    device_ids = jnp.arange(dp_count, dtype=jnp.int32)
    placing = ((device_ids[:, None] // 2 == slot_of[None, :]) & held_here[None, :]).astype(
        jnp.float32
    )
    sources = (block_ids[:, None] // per_group == owner_ids[None, :]).astype(jnp.float32)
    routing = jnp.dot(placing, sources).astype(jnp.bfloat16)
    sectioned = jnp.einsum(
        "ds,src->drc", routing, incoming, preferred_element_type=jnp.float32
    ).astype(jnp.bfloat16)
    full_block = lax.all_to_all(sectioned, "dp", split_axis=0, concat_axis=1, tiled=True)[0]
    parity = dp_where % 2
    oriented = jnp.where(parity == 0, full_block, full_block.T)
    statistic = decay_rate * factors[0, 0] + jnp.dot(
        oriented, oriented.T, preferred_element_type=jnp.float32
    )
    own_root = inverse_root(statistic)
    partner_root = swapped(own_root, "dp", 0)
    left_root = jnp.where(parity == 0, own_root, partner_root)
    right_root = jnp.where(parity == 0, partner_root, own_root)
    half_rows = block_width // 2
    weighted = jnp.dot(left_root, full_block, preferred_element_type=jnp.float32).astype(
        jnp.bfloat16
    )
    weighted_half = lax.dynamic_slice_in_dim(weighted, parity * half_rows, half_rows, 0)
    update = (
        jnp.dot(weighted_half, right_root, preferred_element_type=jnp.float32) * block_width**0.5
    ).astype(jnp.bfloat16)
    return (statistic[None, None], update[None, None])


def solution(mesh):
    placed = (P("dp", "grp"), P("dp", "grp"), P(), P("grp", "dp", None, None))
    return jax.shard_map(
        per_device,
        mesh=mesh,
        in_specs=placed,
        out_specs=(P("grp", "dp", None, None), P("grp", "dp", None, None)),
        check_vma=False,
    )
```

profile of v0, /device:TPU:1, one launch (start us, length us, event | category | flops | bytes accessed | tf_op | source)
XLA Modules:
  0.0 307.0 jit_solution(10898698948101138658)
XLA Ops:
  7.2 0.0 copy-start
  7.2 0.0 copy-start.4
  7.2 0.0 reduce-scatter.2.cloned.1.call-start
  7.2 1.2 copy-done
  8.4 4.1 %convolution_convert_fusion = bf16[512,4096]{1,0:T(8,128)(2,1)} fusion(bf16[128,512]{1,0:T(8,128)(2,1)} %param.4, bf16[128,4096]{1,0:T(8,128)(2,1)S(1)} %copy-done), kind=kOutput, calls=%fused_computation | convolution fusion | flops 538968064 | bytes 5373952 | tf_op jit(solution)/shard_map/dot_general | solution.py:51
  12.5 0.0 reduce-scatter.2.cloned.1.call-update
  12.5 0.0 copy-start.1
  12.5 0.0 copy-done.4
  12.6 0.1 dynamic_slice.6
  12.6 130.0 %reduce-scatter.2.cloned.1.call-done = bf16[16,4096]{1,0:T(8,128)(2,1)} async-done(((bf16[512,4096]{1,0:T(8,128)(2,1)}), bf16[16,4096]{1,0:T(8,128)(2,1)}) %reduce-scatter.2.cloned.1.call-update) | async-done | bytes 131088 | tf_op jit(solution)/shard_map/reduce_scatter | solution.py:50
  142.6 0.9 copy.17
  143.5 0.4 convolution_convert_fusion.3
  144.0 1.1 copy.13
  145.0 28.1 %all-to-all-start = ((bf16[32,16,512]{2,1,0:T(8,128)(2,1)}), bf16[32,16,512]{2,1,0:T(8,128)(2,1)S(1)}, u32[]{:S(2)}, u32[]{:S(2)}) async-start(bf16[32,16,512]{2,1,0:T(8,128)(2,1)} %copy.13), calls=%async_computation.1 | async-start | bytes 1048576 | tf_op jit(solution)/shard_map/all_to_all | solution.py:70
  173.2 0.2 convert_reduce_fusion
  173.4 11.4 %all-to-all-done = bf16[32,16,512]{2,1,0:T(8,128)(2,1)S(1)} async-done(((bf16[32,16,512]{2,1,0:T(8,128)(2,1)}), bf16[32,16,512]{2,1,0:T(8,128)(2,1)S(1)}, u32[]{:S(2)}, u32[]{:S(2)}) %all-to-all-start) | async-done | bytes 524320 | tf_op jit(solution)/shard_map/all_to_all | solution.py:70
  184.8 0.6 convolution_convert_fusion.1
  185.4 1.1 copy.15
  186.4 17.6 %all-to-all-start.1 = ((bf16[32,16,512]{2,1,0:T(8,128)(2,1)}), bf16[32,16,512]{2,1,0:T(8,128)(2,1)S(1)}, u32[]{:S(2)}, u32[]{:S(2)}) async-start(bf16[32,16,512]{2,1,0:T(8,128)(2,1)} %copy.15), calls=%async_computation.2 | async-start | bytes 1048576 | tf_op jit(solution)/shard_map/all_to_all | solution.py:81
  204.1 65.1 %all-to-all-done.1 = bf16[32,16,512]{2,1,0:T(8,128)(2,1)S(1)} async-done(((bf16[32,16,512]{2,1,0:T(8,128)(2,1)}), bf16[32,16,512]{2,1,0:T(8,128)(2,1)S(1)}, u32[]{:S(2)}, u32[]{:S(2)}) %all-to-all-start.1) | async-done | bytes 524320 | tf_op jit(solution)/shard_map/all_to_all | solution.py:81
  269.2 0.2 copy.16
  269.4 0.0 copy-done.1
  269.4 2.1 multiply_reduce_fusion
  272.2 0.0 copy-start.2
  272.2 3.7 %fusion.4 = f32[512,512]{1,0:T(8,128)S(1)} fusion(f32[512,512]{1,0:T(8,128)} %get-tuple-element.3, f32[]{:T(128)S(6)} %sqrt.3), kind=kOutput, calls=%fused_computation.13 | convolution fusion | flops 1611923456 | bytes 2097156 | tf_op jit(solution)/shard_map/dot_general | solution.py:36
  275.8 1.8 fusion.42
  277.7 0.0 copy-done.2
  277.7 0.0 copy-start.3
  277.7 2.9 fusion
  280.6 0.0 copy-done.3
  280.6 3.2 %convolution_convert_fusion.2 = bf16[512,512]{1,0:T(8,128)(2,1)S(1)} fusion(f32[512,512]{1,0:T(8,128)} %fusion, f32[]{:T(128)S(6)} %mul.50, f32[512,512]{1,0:T(8,128)S(1)} %copy-done.3, f32[]{:T(128)S(6)} %sqrt.3), kind=kOutput, calls=%fused_computation.6 | convolution fusion | flops 1612185600 | bytes 2621448 | tf_op jit(solution)/shard_map/dot_general | solution.py:34
  283.8 1.9 collective-permute-start
  285.8 12.9 %collective-permute-done = bf16[512,512]{1,0:T(8,128)(2,1)S(1)} collective-permute-done((bf16[512,512]{1,0:T(8,128)(2,1)S(1)}, bf16[512,512]{1,0:T(8,128)(2,1)S(1)}, u32[]{:S(2)}, u32[]{:S(2)}) %collective-permute-start) | collective-permute-done | bytes 524320 | tf_op jit(solution)/shard_map/ppermute | solution.py:19
  298.7 0.4 fusion.9
  299.1 1.0 fusion.2
  (3 shorter events, 0.0 us)
Async XLA Ops:
  7.2 1.2 copy-start
  7.2 5.4 %copy-start.4 = (s32[256]{0:T(256)S(1)}, s32[256]{0:T(256)}, u32[]{:S(2)}) copy-start(s32[256]{0:T(256)} %param.6) | copy-start | bytes 3076
  7.2 135.4 %reduce-scatter.2.cloned.1.call-start = ((), (), s32[]{:S(2)}) async-start(), calls=%async_computation.3 | async-start | bytes 4325376 | tf_op jit(solution)/shard_map/reduce_scatter | solution.py:50
  12.5 256.9 %copy-start.1 = (f32[1,1,512,512]{3,2,1,0:T(8,128)S(1)}, f32[1,1,512,512]{3,2,1,0:T(8,128)}, u32[]{:S(2)}) copy-start(f32[1,1,512,512]{3,2,1,0:T(8,128)} %param.7) | copy-start | bytes 3145732
  145.0 39.7 %all-to-all-start = ((bf16[32,16,512]{2,1,0:T(8,128)(2,1)}), bf16[32,16,512]{2,1,0:T(8,128)(2,1)S(1)}, u32[]{:S(2)}, u32[]{:S(2)}) async-start(bf16[32,16,512]{2,1,0:T(8,128)(2,1)} %copy.13), calls=%async_computation.1 | async-start | bytes 1048576 | tf_op jit(solution)/shard_map/all_to_all | solution.py:70
  186.4 82.7 %all-to-all-start.1 = ((bf16[32,16,512]{2,1,0:T(8,128)(2,1)}), bf16[32,16,512]{2,1,0:T(8,128)(2,1)S(1)}, u32[]{:S(2)}, u32[]{:S(2)}) async-start(bf16[32,16,512]{2,1,0:T(8,128)(2,1)} %copy.15), calls=%async_computation.2 | async-start | bytes 1048576 | tf_op jit(solution)/shard_map/all_to_all | solution.py:81
  272.2 5.5 %copy-start.2 = (f32[512,512]{1,0:T(8,128)S(1)}, f32[512,512]{1,0:T(8,128)}, u32[]{:S(2)}) copy-start(f32[512,512]{1,0:T(8,128)} %get-tuple-element.3) | copy-start | bytes 3145732
  277.7 2.9 copy-start.3
  283.8 14.9 %collective-permute-start = (bf16[512,512]{1,0:T(8,128)(2,1)S(1)}, bf16[512,512]{1,0:T(8,128)(2,1)S(1)}, u32[]{:S(2)}, u32[]{:S(2)}) collective-permute-start(bf16[512,512]{1,0:T(8,128)(2,1)S(1)} %convolution_convert_fusion.2), channel_id=1, source_target_pairs={{0,32},{32,0},{64,96},{96,64},{128,160},{160,128},{192,224},{224,1... | collective-permute-start | bytes 1572872 | tf_op jit(solution)/shard_map/ppermute | solution.py:19
Sparse Core Ops, SparseCore 0:
  12.6 129.9 reduce-scatter.1
where the time goes:
time: 307 us
  waiting for transfers between devices  219 us (71%)
  starting transfers between devices  47.7 us (16%)
  matrix products  20.1 us (7%)
  between operations  15 us (5%)
  local copies, waits for them, and re-layouts  4.6 us (1%)
    reduce_scatter x1, waiting for transfers between devices, per_device(): lax.psum_scatter(lax.dot_general(acts, grads_out, (((0,), (0,)), ((), ())...  130 us
    all_to_all x1, waiting for transfers between devices, per_device(): lax.all_to_all(sectioned, 'dp', split_axis=0, concat_axis=1, tiled=True)[0]  65.1 us
    all_to_all x1, starting transfers between devices, per_device(): lax.all_to_all(outgoing, 'grp', split_axis=0, concat_axis=0, tiled=True)  28.1 us
    all_to_all x1, starting transfers between devices, per_device(): lax.all_to_all(sectioned, 'dp', split_axis=0, concat_axis=1, tiled=True)[0]  17.6 us
    ppermute x1, waiting for transfers between devices, swapped(): return lax.ppermute(block, axis, route)  12.9 us
    all_to_all x1, waiting for transfers between devices, per_device(): lax.all_to_all(outgoing, 'grp', split_axis=0, concat_axis=0, tiled=True)  11.4 us
  transfers between devices with their start and end apart: 4, of which 4 were waited for; matrix products, arithmetic and copies ran while one was open for 0% of the time, Pallas kernels for 0%

commit v1 on v0

v1 whole, which is shorter than its diff:
```python
import jax
import jax.numpy as jnp
from jax import lax
from jax.experimental import pallas as pl
from jax.experimental.pallas import tpu as pltpu
from jax.sharding import PartitionSpec as P

decay_rate = 0.95
outer_gain = 1.5625
inner_gain = 2.44140625


def swapped(block):
    return lax.ppermute(
        block, "dp", [(place, place ^ 1) for place in range(lax.axis_size("dp"))]
    )


def product(left, right, contract=((1,), (0,))):
    return lax.dot_general(left, right, (contract, ((), ())), preferred_element_type=jnp.float32)


def inverse_root(statistic):
    norm_value = jnp.sqrt(jnp.sum(statistic * statistic))
    first = statistic * (0.2 / norm_value)
    first_low = first.astype(jnp.bfloat16)
    second = product(first_low, first_low)
    third = product(second.astype(jnp.bfloat16), first_low)
    tail = (-10.0 * inner_gain) * first + (5.0 * inner_gain) * second - inner_gain * third
    removed = (
        (1.0 + inner_gain) * first
        - (5.0 * inner_gain) * second
        + (10.0 * inner_gain) * third
        + product(third.astype(jnp.bfloat16), tail.astype(jnp.bfloat16))
    )
    size = statistic.shape[0]
    on_diagonal = lax.broadcasted_iota(jnp.int32, (size, size), 0) == lax.broadcasted_iota(
        jnp.int32, (size, size), 1
    )
    kept = jnp.where(on_diagonal, 1.0, 0.0) - removed
    scale = outer_gain * lax.rsqrt(jnp.sqrt(norm_value))
    return (scale * kept).astype(jnp.bfloat16)


def precondition_kernel(
    parity_ref, own_half, other_half, own_factor, other_factor, statistic_ref, update_ref,
    grad, outer, roots,
):
    parity = parity_ref[0]
    size = grad.shape[0]
    half = size // 2
    grad[:, pl.ds(pl.multiple_of(parity * half, half), half)] = own_half[...]
    grad[:, pl.ds(pl.multiple_of((1 - parity) * half, half), half)] = other_half[...]
    block = grad[...]
    outer[0] = product(block, block, ((1,), (1,)))
    outer[1] = product(block, block, ((0,), (0,)))
    statistic = decay_rate * own_factor[...] + outer[parity]
    statistic_ref[...] = statistic
    roots[parity] = inverse_root(statistic)
    partner = decay_rate * other_factor[...].astype(jnp.float32) + outer[1 - parity]
    roots[1 - parity] = inverse_root(partner)
    left_rows = roots[0, pl.ds(pl.multiple_of(parity * half, half), half), :]
    weighted = product(left_rows, block).astype(jnp.bfloat16)
    update_ref[...] = (product(weighted, roots[1]) * size**0.5).astype(jnp.bfloat16)


def precondition(parity, own_half, other_half, own_factor, other_factor):
    size = own_factor.shape[0]
    in_vmem = pl.BlockSpec(memory_space=pltpu.VMEM)
    return pl.pallas_call(
        precondition_kernel,
        out_shape=(
            jax.ShapeDtypeStruct((size, size), jnp.float32),
            jax.ShapeDtypeStruct((size // 2, size), jnp.bfloat16),
        ),
        in_specs=[pl.BlockSpec(memory_space=pltpu.SMEM)] + [in_vmem] * 4,
        out_specs=(in_vmem, in_vmem),
        scratch_shapes=[
            pltpu.VMEM((size, size), jnp.bfloat16),
            pltpu.VMEM((2, size, size), jnp.float32),
            pltpu.VMEM((2, size, size), jnp.bfloat16),
        ],
        compiler_params=pltpu.CompilerParams(vmem_limit_bytes=40 * 2**20),
        cost_estimate=pl.CostEstimate(
            flops=19 * size**3, bytes_accessed=12 * size**2, transcendentals=0
        ),
    )(parity, own_half, other_half, own_factor, other_factor)


def per_device(acts, grads_out, owner_of, factors):
    dp_count = lax.axis_size("dp")
    grp_count = lax.axis_size("grp")
    tokens, block_width = acts.shape
    half_width = block_width // 2
    per_group = grads_out.shape[1] // block_width
    pair_count = dp_count // 2
    dp_where = lax.axis_index("dp")
    grp_where = lax.axis_index("grp")
    parity = dp_where % 2
    same_parity = [[2 * pair + side for pair in range(pair_count)] for side in range(2)]

    columns = grads_out.reshape(tokens, per_group, 2, half_width)

    def side_of(side):
        taken = lax.dynamic_index_in_dim(columns, side, 2, keepdims=False)
        return taken.reshape(tokens, per_group * half_width)

    sent = jnp.concatenate([acts, side_of(1 - parity)], axis=1)
    received = swapped(sent)
    pair_acts = jnp.concatenate([acts, received[:, :block_width]], axis=0)
    pair_grads = jnp.concatenate([side_of(parity), received[:, block_width:]], axis=0)
    partial_grad = product(pair_acts, pair_grads, ((0,), (0,))).astype(jnp.bfloat16)
    summed = lax.psum_scatter(
        partial_grad, "dp", scatter_dimension=0, tiled=True, axis_index_groups=same_parity
    )
    slab_rows = block_width // pair_count
    grad_rows = summed.reshape(slab_rows, per_group, half_width)

    own_factor = factors[0, 0]
    other_factor = swapped(own_factor.astype(jnp.bfloat16))

    block_count = owner_of.shape[0]
    block_ids = jnp.arange(block_count, dtype=jnp.int32)
    same_owner = owner_of[:, None] == owner_of[None, :]
    earlier = block_ids[None, :] < block_ids[:, None]
    slot_of = jnp.sum((same_owner & earlier).astype(jnp.int32), axis=1)
    owner_ids = jnp.arange(grp_count, dtype=jnp.int32)
    local_owners = lax.dynamic_slice_in_dim(owner_of, grp_where * per_group, per_group)
    chooser = (owner_ids[:, None] == local_owners[None, :]).astype(jnp.bfloat16)
    outgoing = jnp.einsum(
        "oj,sjc->osc", chooser, grad_rows, preferred_element_type=jnp.float32
    ).astype(jnp.bfloat16)
    incoming = lax.all_to_all(outgoing, "grp", split_axis=0, concat_axis=0, tiled=True)
    held_here = owner_of == grp_where
    slot_ids = jnp.arange(pair_count, dtype=jnp.int32)
    placing = ((slot_ids[:, None] == slot_of[None, :]) & held_here[None, :]).astype(jnp.float32)
    sources = (block_ids[:, None] // per_group == owner_ids[None, :]).astype(jnp.float32)
    routing = jnp.dot(placing, sources).astype(jnp.bfloat16)
    sectioned = jnp.einsum(
        "ks,src->krc", routing, incoming, preferred_element_type=jnp.float32
    ).astype(jnp.bfloat16)
    own_half = lax.all_to_all(
        sectioned, "dp", split_axis=0, concat_axis=0, tiled=True, axis_index_groups=same_parity
    ).reshape(block_width, half_width)
    other_half = swapped(own_half)
    statistic, update = precondition(
        parity.astype(jnp.int32).reshape(1), own_half, other_half, own_factor, other_factor
    )
    return (statistic[None, None], update[None, None])


def solution(mesh):
    placed = (P("dp", "grp"), P("dp", "grp"), P(), P("grp", "dp", None, None))
    return jax.shard_map(
        per_device,
        mesh=mesh,
        in_specs=placed,
        out_specs=(P("grp", "dp", None, None), P("grp", "dp", None, None)),
        check_vma=False,
    )
```

time: 307 us -> 234 us (0.76)
  waiting for transfers between devices: 219 us -> 158 us
  matrix products: 20.1 us -> 3.25 us
  Pallas kernels: 0 us -> 5.05 us
    all_to_all x1, waiting for transfers between devices: 65.1 us -> 22.4 us  [per_device(): lax.all_to_all(sectioned, 'dp', split_axis=0, concat_axis=0, tiled=True,...]
    reduce_scatter x1, waiting for transfers between devices: 130 us -> 111 us  [per_device(): lax.psum_scatter(partial_grad, 'dp', scatter_dimension=0, tiled=True, axi...]
    ppermute x1 -> x3, starting transfers between devices: 1.92 us -> 20.2 us  [swapped(): lax.ppermute(block, 'dp', [(place, place ^ 1) for place in range(lax.axis...]
    dot_general x9 -> x2, matrix products: 19.7 us -> 2.85 us  [the longest x1 2.09 us: product(): lax.dot_general(left, right, (contract, ((), ())), preferred_element_type...]
    all_to_all x1, starting transfers between devices: 28.1 us -> 16.8 us  [per_device(): lax.all_to_all(outgoing, 'grp', split_axis=0, concat_axis=0, tiled=True)]
    all_to_all x1, starting transfers between devices: 17.6 us -> 8.53 us  [per_device(): lax.all_to_all(sectioned, 'dp', split_axis=0, concat_axis=0, tiled=True,...]
    pallas_call x0 -> x1, Pallas kernels: none -> 5.05 us  [precondition(): pl.pallas_call(precondition_kernel, out_shape=(jax.ShapeDtypeStruct((size...]
    ppermute x1 -> x3, waiting for transfers between devices: 12.9 us -> 13.1 us  [swapped(): lax.ppermute(block, 'dp', [(place, place ^ 1) for place in range(lax.axis...]
  transfers between devices with their start and end apart: 4 -> 6, of which waited for: 4 -> 5; matrix products, arithmetic and copies ran while one was open for 0% -> 0% of each run, Pallas kernels for 0% -> 0%
where the time goes in v1:
time: 234 us; the launch traced here: 232 us
  waiting for transfers between devices  158 us (68%)
  starting transfers between devices  45.6 us (19%)
  between operations  14.2 us (6%)
  Pallas kernels  5.05 us (2%)
  local copies, waits for them, and re-layouts  4.76 us (2%)
  matrix products  3.25 us (1%)
    reduce_scatter x1, waiting for transfers between devices, per_device(): lax.psum_scatter(partial_grad, 'dp', scatter_dimension=0, tiled=True, axi...  111 us
    all_to_all x1, waiting for transfers between devices, per_device(): lax.all_to_all(sectioned, 'dp', split_axis=0, concat_axis=0, tiled=True,...  22.4 us
    ppermute x3, starting transfers between devices, swapped(): lax.ppermute(block, 'dp', [(place, place ^ 1) for place in range(lax.axis...  20.2 us
    all_to_all x1, starting transfers between devices, per_device(): lax.all_to_all(outgoing, 'grp', split_axis=0, concat_axis=0, tiled=True)  16.8 us
    ppermute x3, waiting for transfers between devices, swapped(): lax.ppermute(block, 'dp', [(place, place ^ 1) for place in range(lax.axis...  13.1 us
    all_to_all x1, waiting for transfers between devices, per_device(): lax.all_to_all(outgoing, 'grp', split_axis=0, concat_axis=0, tiled=True)  11.4 us
    all_to_all x1, starting transfers between devices, per_device(): lax.all_to_all(sectioned, 'dp', split_axis=0, concat_axis=0, tiled=True,...  8.53 us
    pallas_call x1, Pallas kernels, precondition(): pl.pallas_call(precondition_kernel, out_shape=(jax.ShapeDtypeStruct((size...  5.05 us
  transfers between devices with their start and end apart: 6, of which 5 were waited for; matrix products, arithmetic and copies ran while one was open for 0% of the time, Pallas kernels for 0%

profile of v1, /device:TPU:1, one launch (start us, length us, event | category | flops | bytes accessed | tf_op | source)
XLA Modules:
  0.0 231.5 jit_solution(1276684262764339589)
XLA Ops:
  7.2 0.0 copy-start.1
  7.2 0.0 reduce-scatter.2.cloned.1.call-start
  7.2 1.6 copy.20
  8.9 0.0 copy-done.1
  8.9 0.1 copy.22
  9.0 0.1 constant_dynamic-slice_fusion
  9.1 4.4 %collective-permute-start = (bf16[128,2560]{0,1:T(8,128)(2,1)S(1)}, bf16[128,2560]{0,1:T(8,128)(2,1)S(1)}, u32[]{:S(2)}, u32[]{:S(2)}) collective-permute-start(bf16[128,2560]{0,1:T(8,128)(2,1)S(1)} %pad_maximum_fusion), channel_id=1, source_target_pairs={{0,32},{32,0},{64,96},{96,64},{128,160},{160,128},{192,224},{224,1... | collective-permute-start | bytes 1966088 | tf_op jit(solution)/shard_map/ppermute | solution.py:14
  13.5 8.0 %collective-permute-done = bf16[128,2560]{0,1:T(8,128)(2,1)S(1)} collective-permute-done((bf16[128,2560]{0,1:T(8,128)(2,1)S(1)}, bf16[128,2560]{0,1:T(8,128)(2,1)S(1)}, u32[]{:S(2)}, u32[]{:S(2)}) %collective-permute-start) | collective-permute-done | bytes 655392 | tf_op jit(solution)/shard_map/ppermute | solution.py:14
  21.5 0.0 copy-start.2
  21.6 2.1 convolution_convert_fusion
  23.6 0.0 reduce-scatter.2.cloned.1.call-update
  23.7 0.0 copy-done.2
  23.7 0.1 dynamic_slice.10
  23.8 111.4 %reduce-scatter.2.cloned.1.call-done = bf16[32,2048]{1,0:T(8,128)(2,1)} async-done(((bf16[512,2048]{1,0:T(8,128)(2,1)}), bf16[32,2048]{1,0:T(8,128)(2,1)}) %reduce-scatter.2.cloned.1.call-update) | async-done | bytes 131088 | tf_op jit(solution)/shard_map/reduce_scatter | solution.py:113
  135.2 0.9 copy.26
  136.1 0.4 convolution_convert_fusion.1
  136.5 0.0 copy-start
  136.5 1.1 copy.23
  137.6 16.8 %all-to-all-start = ((bf16[32,32,256]{2,1,0:T(8,128)(2,1)}), bf16[32,32,256]{2,1,0:T(8,128)(2,1)S(1)}, u32[]{:S(2)}, u32[]{:S(2)}) async-start(bf16[32,32,256]{2,1,0:T(8,128)(2,1)} %copy.23), calls=%async_computation.1 | async-start | bytes 1048576 | tf_op jit(solution)/shard_map/all_to_all | solution.py:133
  154.5 0.2 convert_reduce_fusion
  154.7 11.4 %all-to-all-done = bf16[32,32,256]{2,1,0:T(8,128)(2,1)S(1)} async-done(((bf16[32,32,256]{2,1,0:T(8,128)(2,1)}), bf16[32,32,256]{2,1,0:T(8,128)(2,1)S(1)}, u32[]{:S(2)}, u32[]{:S(2)}) %all-to-all-start) | async-done | bytes 524320 | tf_op jit(solution)/shard_map/all_to_all | solution.py:133
  166.1 0.8 convolution_convert_fusion.2
  166.9 0.8 copy.25
  167.7 8.5 %all-to-all-start.1 = ((bf16[16,32,256]{2,1,0:T(8,128)(2,1)}), bf16[16,32,256]{2,1,0:T(8,128)(2,1)S(1)}, u32[]{:S(2)}, u32[]{:S(2)}) async-start(bf16[16,32,256]{2,1,0:T(8,128)(2,1)} %copy.25), calls=%async_computation.2 | async-start | bytes 524288 | tf_op jit(solution)/shard_map/all_to_all | solution.py:142
  176.2 0.0 copy-done
  176.2 0.1 bitcast_convert_fusion
  176.3 3.6 %collective-permute-start.2 = (bf16[512,512]{1,0:T(8,128)(2,1)S(1)}, bf16[512,512]{1,0:T(8,128)(2,1)S(1)}, u32[]{:S(2)}, u32[]{:S(2)}) collective-permute-start(bf16[512,512]{1,0:T(8,128)(2,1)S(1)} %bitcast_convert_fusion), channel_id=1, source_target_pairs={{0,32},{32,0},{64,96},{96,64},{128,160},{160,128},{192,224},{224,1... | collective-permute-start | bytes 1572872 | tf_op jit(solution)/shard_map/ppermute | solution.py:14
  179.8 22.4 %all-to-all-done.1 = bf16[16,32,256]{2,1,0:T(8,128)(2,1)S(1)} async-done(((bf16[16,32,256]{2,1,0:T(8,128)(2,1)}), bf16[16,32,256]{2,1,0:T(8,128)(2,1)S(1)}, u32[]{:S(2)}, u32[]{:S(2)}) %all-to-all-start.1) | async-done | bytes 262176 | tf_op jit(solution)/shard_map/all_to_all | solution.py:142
  202.3 12.2 %collective-permute-start.1 = (bf16[512,256]{1,0:T(8,128)(2,1)S(1)}, bf16[512,256]{1,0:T(8,128)(2,1)S(1)}, u32[]{:S(2)}, u32[]{:S(2)}) collective-permute-start(bf16[512,256]{1,0:T(8,128)(2,1)S(1)} %bitcast.20), channel_id=1, source_target_pairs={{0,32},{32,0},{64,96},{96,64},{128,160},{160,128},{192,224},{224,1... | collective-permute-start | bytes 786440 | tf_op jit(solution)/shard_map/ppermute | solution.py:14
  214.5 0.0 collective-permute-done.2.other_factor
  214.5 5.1 %collective-permute-done.1.other_half = bf16[512,256]{1,0:T(8,128)(2,1)S(1)} collective-permute-done((bf16[512,256]{1,0:T(8,128)(2,1)S(1)}, bf16[512,256]{1,0:T(8,128)(2,1)S(1)}, u32[]{:S(2)}, u32[]{:S(2)}) %collective-permute-start.1) | collective-permute-done | bytes 262176 | tf_op jit(solution)/shard_map/ppermute | solution.py:14
  219.6 5.1 %shard_map.59 = (f32[512,512]{1,0:T(8,128)}, bf16[256,512]{1,0:T(8,128)(2,1)}) custom-call(s32[1]{0:T(128)} %bitcast.parity_ref, bf16[512,256]{1,0:T(8,128)(2,1)S(1)} %bitcast.21, bf16[512,256]{1,0:T(8,128)(2,1)S(1)} %collective-permute-done.1.other_half, f32[512,512]{1,0:T(8,128)S(1)} %bitcast.19, bf16[512,512]{1,0:T(8,128)(2,1)S(1)} %collective-permute-done.2.other_factor), custom_call_target="tpu_custom_call" | custom-call | flops 2550136832 | bytes 3145728 | tf_op jit(solution)/shard_map/pallas_call | solution.py:70
  (5 shorter events, 0.1 us)
Async XLA Ops:
  7.2 1.7 copy-start.1
  7.2 128.0 %reduce-scatter.2.cloned.1.call-start = ((), (), s32[]{:S(2)}) async-start(), calls=%async_computation.3 | async-start | bytes 2228224 | tf_op jit(solution)/shard_map/reduce_scatter | solution.py:113
  9.1 12.3 %collective-permute-start = (bf16[128,2560]{0,1:T(8,128)(2,1)S(1)}, bf16[128,2560]{0,1:T(8,128)(2,1)S(1)}, u32[]{:S(2)}, u32[]{:S(2)}) collective-permute-start(bf16[128,2560]{0,1:T(8,128)(2,1)S(1)} %pad_maximum_fusion), channel_id=1, source_target_pairs={{0,32},{32,0},{64,96},{96,64},{128,160},{160,128},{192,224},{224,1... | collective-permute-start | bytes 1966088 | tf_op jit(solution)/shard_map/ppermute | solution.py:14
  21.5 2.1 copy-start.2
  136.5 39.7 %copy-start = (f32[1,1,512,512]{3,2,1,0:T(8,128)S(1)}, f32[1,1,512,512]{3,2,1,0:T(8,128)}, u32[]{:S(2)}) copy-start(f32[1,1,512,512]{3,2,1,0:T(8,128)} %param.7) | copy-start | bytes 3145732
  137.6 28.5 %all-to-all-start = ((bf16[32,32,256]{2,1,0:T(8,128)(2,1)}), bf16[32,32,256]{2,1,0:T(8,128)(2,1)S(1)}, u32[]{:S(2)}, u32[]{:S(2)}) async-start(bf16[32,32,256]{2,1,0:T(8,128)(2,1)} %copy.23), calls=%async_computation.1 | async-start | bytes 1048576 | tf_op jit(solution)/shard_map/all_to_all | solution.py:133
  167.7 34.6 %all-to-all-start.1 = ((bf16[16,32,256]{2,1,0:T(8,128)(2,1)}), bf16[16,32,256]{2,1,0:T(8,128)(2,1)S(1)}, u32[]{:S(2)}, u32[]{:S(2)}) async-start(bf16[16,32,256]{2,1,0:T(8,128)(2,1)} %copy.25), calls=%async_computation.2 | async-start | bytes 524288 | tf_op jit(solution)/shard_map/all_to_all | solution.py:142
  176.3 38.2 %collective-permute-start.2 = (bf16[512,512]{1,0:T(8,128)(2,1)S(1)}, bf16[512,512]{1,0:T(8,128)(2,1)S(1)}, u32[]{:S(2)}, u32[]{:S(2)}) collective-permute-start(bf16[512,512]{1,0:T(8,128)(2,1)S(1)} %bitcast_convert_fusion), channel_id=1, source_target_pairs={{0,32},{32,0},{64,96},{96,64},{128,160},{160,128},{192,224},{224,1... | collective-permute-start | bytes 1572872 | tf_op jit(solution)/shard_map/ppermute | solution.py:14
  202.3 17.4 %collective-permute-start.1 = (bf16[512,256]{1,0:T(8,128)(2,1)S(1)}, bf16[512,256]{1,0:T(8,128)(2,1)S(1)}, u32[]{:S(2)}, u32[]{:S(2)}) collective-permute-start(bf16[512,256]{1,0:T(8,128)(2,1)S(1)} %bitcast.20), channel_id=1, source_target_pairs={{0,32},{32,0},{64,96},{96,64},{128,160},{160,128},{192,224},{224,1... | collective-permute-start | bytes 786440 | tf_op jit(solution)/shard_map/ppermute | solution.py:14
Sparse Core Ops, SparseCore 0:
  23.8 111.3 reduce-scatter.1

commit v2 on v1

--- a/solution.py
+++ b/solution.py
@@ -10,9 +10,19 @@
 inner_gain = 2.44140625
 
 
-def swapped(block):
+team = 4
+
+
+def across(block, mask):
     return lax.ppermute(
-        block, "dp", [(place, place ^ 1) for place in range(lax.axis_size("dp"))]
+        block, "dp", [(place, place ^ mask) for place in range(lax.axis_size("dp"))]
+    )
+
+
+def along(block, distance):
+    count = lax.axis_size("dp")
+    return lax.ppermute(
+        block, "dp", [(place, (place + distance) % count) for place in range(count)]
     )
 
 
@@ -49,8 +59,11 @@
     parity = parity_ref[0]
     size = grad.shape[0]
     half = size // 2
-    grad[:, pl.ds(pl.multiple_of(parity * half, half), half)] = own_half[...]
-    grad[:, pl.ds(pl.multiple_of((1 - parity) * half, half), half)] = other_half[...]
+    pieces, rows, width = own_half.shape
+    for piece in range(pieces):
+        at = piece // 2 * rows
+        for side, source in ((parity, own_half), (1 - parity, other_half)):
+            grad[at : at + rows, wide(2 * side + piece % 2, width)] = source[piece]
     block = grad[...]
     outer[0] = product(block, block, ((1,), (1,)))
     outer[1] = product(block, block, ((0,), (0,)))
@@ -87,37 +100,162 @@
     )(parity, own_half, other_half, own_factor, other_factor)
 
 
+def in_vmem():
+    return pl.BlockSpec(memory_space=pltpu.VMEM)
+
+
+def in_smem():
+    return pl.BlockSpec(memory_space=pltpu.SMEM)
+
+
+def wide(place, width):
+    return pl.ds(pl.multiple_of(place * width, width), width)
+
+
+def quarter_of(member):
+    return 2 * (member % 2) + member // 2
+
+
+def send_kernel(member_ref, acts_ref, grads_ref, *sent_refs):
+    block_width = acts_ref.shape[1]
+    width = block_width // team
+    for mask, sent_ref in zip((2, 3, 1), sent_refs):
+        quarter = quarter_of(member_ref[0] ^ mask)
+        sent_ref[:, :block_width] = acts_ref[...]
+        for block in range(grads_ref.shape[1] // block_width):
+            at = block_width + block * width
+            sent_ref[:, at : at + width] = grads_ref[:, wide(team * block + quarter, width)]
+
+
+def team_messages(member, acts, grads_out):
+    tokens, block_width = acts.shape
+    message = jax.ShapeDtypeStruct(
+        (tokens, block_width + grads_out.shape[1] // team), acts.dtype
+    )
+    return pl.pallas_call(
+        send_kernel,
+        out_shape=(message,) * 3,
+        in_specs=[in_smem(), in_vmem(), in_vmem()],
+        out_specs=(in_vmem(),) * 3,
+        compiler_params=pltpu.CompilerParams(vmem_limit_bytes=24 * 2**20),
+    )(member, acts, grads_out)
+
+
+def gradient_kernel(
+    member_ref, place_ref, acts_ref, grads_ref, first, second, third, partial_ref, whole
+):
+    block_width = acts_ref.shape[1]
+    width = block_width // team
+    messages = (first, second, third)
+    quarter = quarter_of(member_ref[0])
+    inputs = jnp.concatenate(
+        [acts_ref[...]] + [message[:, :block_width] for message in messages], axis=0
+    )
+    blocks = grads_ref.shape[1] // block_width
+    for pair in range(0, blocks, 2):
+        own = jnp.concatenate(
+            [grads_ref[:, wide(team * block + quarter, width)] for block in (pair, pair + 1)],
+            axis=1,
+        )
+        at = block_width + pair * width
+        cotangents = jnp.concatenate(
+            [own] + [message[:, at : at + 2 * width] for message in messages], axis=0
+        )
+        whole[:, pair * width : (pair + 2) * width] = product(
+            inputs, cotangents, ((0,), (0,))
+        ).astype(whole.dtype)
+    stops, rows, _ = partial_ref.shape
+    for ahead in range(stops):
+        stop = lax.rem(place_ref[0] + ahead, stops)
+        partial_ref[ahead] = whole[wide(stop, rows), :]
+
+
+def team_gradient(member, place, stops, acts, grads_out, messages):
+    tokens, block_width = acts.shape
+    columns = grads_out.shape[1] // team
+    return pl.pallas_call(
+        gradient_kernel,
+        out_shape=jax.ShapeDtypeStruct((stops, block_width // stops, columns), jnp.bfloat16),
+        in_specs=[in_smem()] * 2 + [in_vmem()] * 5,
+        out_specs=in_vmem(),
+        scratch_shapes=[pltpu.VMEM((block_width, columns), jnp.bfloat16)],
+        compiler_params=pltpu.CompilerParams(vmem_limit_bytes=32 * 2**20),
+        cost_estimate=pl.CostEstimate(
+            flops=2 * team * tokens * block_width * columns,
+            bytes_accessed=2**22,
+            transcendentals=0,
+        ),
+    )(member, place, acts, grads_out, *messages)
+
+
+def plus(left, right):
+    return (left.astype(jnp.float32) + right.astype(jnp.float32)).astype(left.dtype)
+
+
+def ring_terms(partial):
+    stops = partial.shape[0]
+    terms = [partial[0]]
+    for step, length in ((1, stops // 2), (-1, stops - 1 - stops // 2)):
+        if length:
+            chain = partial[step * length % stops]
+            for left in range(length - 1, -1, -1):
+                chain = along(chain, step * team)
+                if left:
+                    chain = plus(chain, partial[step * left % stops])
+            terms.append(chain)
+    return terms
+
+
+def outgoing_kernel(chosen_ref, *refs):
+    *term_refs, out_ref, rows = refs
+    rows[...] = sum(term[...].astype(jnp.float32) for term in term_refs).astype(rows.dtype)
+    width = out_ref.shape[2]
+    for owner in range(out_ref.shape[0]):
+        out_ref[owner] = rows[:, wide(chosen_ref[owner], width)]
+
+
+def by_owner(chosen, terms, width):
+    rows, columns = terms[0].shape
+    return pl.pallas_call(
+        outgoing_kernel,
+        out_shape=jax.ShapeDtypeStruct((chosen.shape[0], rows, width), terms[0].dtype),
+        in_specs=[in_smem()] + [in_vmem()] * len(terms),
+        out_specs=in_vmem(),
+        scratch_shapes=[pltpu.VMEM((rows, columns), terms[0].dtype)],
+        compiler_params=pltpu.CompilerParams(vmem_limit_bytes=16 * 2**20),
+    )(chosen, *terms)
+
+
+def slot_kernel(source_ref, incoming_ref, out_ref):
+    for slot in range(out_ref.shape[0]):
+        source = source_ref[slot]
+        piece = incoming_ref[jnp.maximum(source, 0)]
+        out_ref[slot] = jnp.where(source >= 0, piece, jnp.zeros_like(piece))
+
+
+def by_slot(source, incoming):
+    return pl.pallas_call(
+        slot_kernel,
+        out_shape=jax.ShapeDtypeStruct(
+            (source.shape[0],) + incoming.shape[1:], incoming.dtype
+        ),
+        in_specs=[in_smem(), in_vmem()],
+        out_specs=in_vmem(),
+        compiler_params=pltpu.CompilerParams(vmem_limit_bytes=16 * 2**20),
+    )(source, incoming)
+
+
 def per_device(acts, grads_out, owner_of, factors):
     dp_count = lax.axis_size("dp")
     grp_count = lax.axis_size("grp")
-    tokens, block_width = acts.shape
-    half_width = block_width // 2
+    block_width = acts.shape[1]
     per_group = grads_out.shape[1] // block_width
     pair_count = dp_count // 2
-    dp_where = lax.axis_index("dp")
     grp_where = lax.axis_index("grp")
-    parity = dp_where % 2
+    stops = dp_count // team
+    dp_where = lax.axis_index("dp").astype(jnp.int32).reshape(1)
+    parity, member, place = dp_where % 2, dp_where % team, dp_where // team
     same_parity = [[2 * pair + side for pair in range(pair_count)] for side in range(2)]
-
-    columns = grads_out.reshape(tokens, per_group, 2, half_width)
-
-    def side_of(side):
-        taken = lax.dynamic_index_in_dim(columns, side, 2, keepdims=False)
-        return taken.reshape(tokens, per_group * half_width)
-
-    sent = jnp.concatenate([acts, side_of(1 - parity)], axis=1)
-    received = swapped(sent)
-    pair_acts = jnp.concatenate([acts, received[:, :block_width]], axis=0)
-    pair_grads = jnp.concatenate([side_of(parity), received[:, block_width:]], axis=0)
-    partial_grad = product(pair_acts, pair_grads, ((0,), (0,))).astype(jnp.bfloat16)
-    summed = lax.psum_scatter(
-        partial_grad, "dp", scatter_dimension=0, tiled=True, axis_index_groups=same_parity
-    )
-    slab_rows = block_width // pair_count
-    grad_rows = summed.reshape(slab_rows, per_group, half_width)
-
-    own_factor = factors[0, 0]
-    other_factor = swapped(own_factor.astype(jnp.bfloat16))
 
     block_count = owner_of.shape[0]
     block_ids = jnp.arange(block_count, dtype=jnp.int32)
@@ -126,26 +264,34 @@
     slot_of = jnp.sum((same_owner & earlier).astype(jnp.int32), axis=1)
     owner_ids = jnp.arange(grp_count, dtype=jnp.int32)
     local_owners = lax.dynamic_slice_in_dim(owner_of, grp_where * per_group, per_group)
-    chooser = (owner_ids[:, None] == local_owners[None, :]).astype(jnp.bfloat16)
-    outgoing = jnp.einsum(
-        "oj,sjc->osc", chooser, grad_rows, preferred_element_type=jnp.float32
-    ).astype(jnp.bfloat16)
+    local_ids = jnp.arange(per_group, dtype=jnp.int32)
+    chosen = jnp.max(
+        jnp.where(owner_ids[:, None] == local_owners[None, :], local_ids[None, :], 0), axis=1
+    )
+    slot_ids = jnp.arange(pair_count, dtype=jnp.int32)
+    placing = (slot_ids[:, None] == slot_of[None, :]) & (owner_of == grp_where)[None, :]
+    source = jnp.max(jnp.where(placing, block_ids[None, :] // per_group, -1), axis=1)
+
+    sent = team_messages(member, acts, grads_out)
+    messages = [across(message, mask) for mask, message in zip((2, 3, 1), sent)]
+    terms = ring_terms(team_gradient(member, place, stops, acts, grads_out, messages))
+    own_factor = factors[0, 0]
+    outgoing, factor_low = lax.optimization_barrier(
+        (by_owner(chosen, terms, block_width // team), own_factor.astype(jnp.bfloat16))
+    )
+    other_factor = across(factor_low, 1)
     incoming = lax.all_to_all(outgoing, "grp", split_axis=0, concat_axis=0, tiled=True)
-    held_here = owner_of == grp_where
-    slot_ids = jnp.arange(pair_count, dtype=jnp.int32)
-    placing = ((slot_ids[:, None] == slot_of[None, :]) & held_here[None, :]).astype(jnp.float32)
-    sources = (block_ids[:, None] // per_group == owner_ids[None, :]).astype(jnp.float32)
-    routing = jnp.dot(placing, sources).astype(jnp.bfloat16)
-    sectioned = jnp.einsum(
-        "ks,src->krc", routing, incoming, preferred_element_type=jnp.float32
-    ).astype(jnp.bfloat16)
+    incoming, other_factor = lax.optimization_barrier((incoming, other_factor))
     own_half = lax.all_to_all(
-        sectioned, "dp", split_axis=0, concat_axis=0, tiled=True, axis_index_groups=same_parity
-    ).reshape(block_width, half_width)
-    other_half = swapped(own_half)
-    statistic, update = precondition(
-        parity.astype(jnp.int32).reshape(1), own_half, other_half, own_factor, other_factor
-    )
+        by_slot(source, incoming),
+        "dp",
+        split_axis=0,
+        concat_axis=0,
+        tiled=True,
+        axis_index_groups=same_parity,
+    )
+    other_half = across(own_half, 1)
+    statistic, update = precondition(parity, own_half, other_half, own_factor, other_factor)
     return (statistic[None, None], update[None, None])
 
 

time: 234 us -> 213 us (0.910)
  waiting for transfers between devices: 158 us -> 67.9 us
  blocking collectives: 0 us -> 48.7 us
  starting transfers between devices: 45.6 us -> 79.9 us
  between operations: 14.2 us -> 0.89 us
  Pallas kernels: 5.05 us -> 8.31 us
  matrix products: 3.25 us -> 0 us
    reduce_scatter x1 -> x0, waiting for transfers between devices: 111 us -> none  [per_device(): lax.psum_scatter(partial_grad, 'dp', scatter_dimension=0, tiled=True, axi...]
    all_to_all x0 -> x1, blocking collectives: none -> 48.7 us  [per_device(): lax.all_to_all(by_slot(source, incoming), 'dp', split_axis=0, concat_axis...]
    ppermute x3 -> x12, starting transfers between devices: 20.2 us -> 66.9 us  [the longest x7 43.4 us: along(): lax.ppermute(block, 'dp', [(place, (place + distance) % count) for place...]
    ppermute x3 -> x12, waiting for transfers between devices: 13.1 us -> 56.6 us  [the longest x7 28.6 us: along(): lax.ppermute(block, 'dp', [(place, (place + distance) % count) for place...]
    all_to_all x1 -> x0, waiting for transfers between devices: 22.4 us -> none  [per_device(): lax.all_to_all(sectioned, 'dp', split_axis=0, concat_axis=0, tiled=True,...]
    all_to_all x1 -> x0, starting transfers between devices: 8.53 us -> none  [per_device(): lax.all_to_all(sectioned, 'dp', split_axis=0, concat_axis=0, tiled=True,...]
    all_to_all x1, starting transfers between devices: 16.8 us -> 13 us  [per_device(): lax.all_to_all(outgoing, 'grp', split_axis=0, concat_axis=0, tiled=True)]
    dot_general x3 -> x0, matrix products: 3.25 us -> none  [the longest x1 2.09 us: product(): lax.dot_general(left, right, (contract, ((), ())), preferred_element_type...]
  transfers between devices with their start and end apart: 6 -> 13, of which waited for: 5 -> 9; matrix products, arithmetic and copies ran while one was open for 0% -> 0% of each run, Pallas kernels for 0% -> 0%
where the time goes in v2:
time: 213 us; the launch traced here: 209 us
  starting transfers between devices  79.9 us (38%)
  waiting for transfers between devices  67.9 us (32%)
  blocking collectives  48.7 us (23%)
  Pallas kernels  8.31 us (4%)
  local copies, waits for them, and re-layouts  2.91 us (1%)
    all_to_all x1, blocking collectives, per_device(): lax.all_to_all(by_slot(source, incoming), 'dp', split_axis=0, concat_axis...  48.7 us
    ppermute x7, starting transfers between devices, along(): lax.ppermute(block, 'dp', [(place, (place + distance) % count) for place...  43.4 us
    ppermute x7, waiting for transfers between devices, along(): lax.ppermute(block, 'dp', [(place, (place + distance) % count) for place...  28.6 us
    ppermute x5, waiting for transfers between devices, across(): lax.ppermute(block, 'dp', [(place, place ^ mask) for place in range(lax.a...  28 us
    ppermute x5, starting transfers between devices, across(): lax.ppermute(block, 'dp', [(place, place ^ mask) for place in range(lax.a...  23.5 us
    all_to_all x1, starting transfers between devices, per_device(): lax.all_to_all(outgoing, 'grp', split_axis=0, concat_axis=0, tiled=True)  13 us
    all_to_all x1, waiting for transfers between devices, per_device(): lax.all_to_all(outgoing, 'grp', split_axis=0, concat_axis=0, tiled=True)  11.3 us
    pallas_call x1, Pallas kernels, precondition(): pl.pallas_call(precondition_kernel, out_shape=(jax.ShapeDtypeStruct((size...  5.11 us
  transfers between devices with their start and end apart: 13, of which 9 were waited for; matrix products, arithmetic and copies ran while one was open for 0% of the time, Pallas kernels for 0%

profile of v2, /device:TPU:1, one launch (start us, length us, event | category | flops | bytes accessed | tf_op | source)
XLA Modules:
  0.0 209.2 jit_solution(6616864080776194238)
XLA Ops:
  0.6 0.0 copy-start
  0.7 1.2 copy-done
  1.9 0.9 copy-done.3
  2.8 0.2 shard_map.59
  3.0 5.9 %collective-permute-start = (bf16[128,1536]{1,0:T(8,128)(2,1)S(1)}, bf16[128,1536]{1,0:T(8,128)(2,1)S(1)}, u32[]{:S(2)}, u32[]{:S(2)}) collective-permute-start(bf16[128,1536]{1,0:T(8,128)(2,1)S(1)} %get-tuple-element.11), channel_id=1, source_target_pairs={{0,64},{32,96},{64,0},{96,32},{128,192},{160,224},{192,128},{224,1... | collective-permute-start | bytes 1179656 | tf_op jit(solution)/shard_map/ppermute | solution.py:17
  8.9 3.3 %collective-permute-start.1 = (bf16[128,1536]{1,0:T(8,128)(2,1)S(1)}, bf16[128,1536]{1,0:T(8,128)(2,1)S(1)}, u32[]{:S(2)}, u32[]{:S(2)}) collective-permute-start(bf16[128,1536]{1,0:T(8,128)(2,1)S(1)} %get-tuple-element.12), channel_id=1, source_target_pairs={{0,96},{32,64},{64,32},{96,0},{128,224},{160,192},{192,160},{224,1... | collective-permute-start | bytes 1179656 | tf_op jit(solution)/shard_map/ppermute | solution.py:17
  12.2 2.2 %collective-permute-start.2 = (bf16[128,1536]{1,0:T(8,128)(2,1)S(1)}, bf16[128,1536]{1,0:T(8,128)(2,1)S(1)}, u32[]{:S(2)}, u32[]{:S(2)}) collective-permute-start(bf16[128,1536]{1,0:T(8,128)(2,1)S(1)} %get-tuple-element.13), channel_id=1, source_target_pairs={{0,32},{32,0},{64,96},{96,64},{128,160},{160,128},{192,224},{224,1... | collective-permute-start | bytes 1179656 | tf_op jit(solution)/shard_map/ppermute | solution.py:17
  14.4 19.5 %collective-permute-done.first = bf16[128,1536]{1,0:T(8,128)(2,1)S(1)} collective-permute-done((bf16[128,1536]{1,0:T(8,128)(2,1)S(1)}, bf16[128,1536]{1,0:T(8,128)(2,1)S(1)}, u32[]{:S(2)}, u32[]{:S(2)}) %collective-permute-start) | collective-permute-done | bytes 393248 | tf_op jit(solution)/shard_map/ppermute | solution.py:17
  33.9 0.0 collective-permute-done.1.second
  33.9 3.3 %collective-permute-done.2.third = bf16[128,1536]{1,0:T(8,128)(2,1)S(1)} collective-permute-done((bf16[128,1536]{1,0:T(8,128)(2,1)S(1)}, bf16[128,1536]{1,0:T(8,128)(2,1)S(1)}, u32[]{:S(2)}, u32[]{:S(2)}) %collective-permute-start.2) | collective-permute-done | bytes 393248 | tf_op jit(solution)/shard_map/ppermute | solution.py:17
  37.2 0.0 copy-done.1
  37.2 0.0 copy-done.4
  37.2 0.8 shard_map.60
  38.1 0.0 copy-start.2
  38.1 10.9 %collective-permute-start.3 = (bf16[64,1024]{1,0:T(8,128)(2,1)S(1)}, bf16[64,1024]{1,0:T(8,128)(2,1)S(1)}, u32[]{:S(2)}, u32[]{:S(2)}) collective-permute-start(bf16[64,1024]{1,0:T(8,128)(2,1)S(1)} %get-tuple-element.25), channel_id=1, source_target_pairs={{0,128},{32,160},{64,192},{96,224},{128,256},{160,288},{192,320},{... | collective-permute-start | bytes 393224 | tf_op jit(solution)/shard_map/ppermute | solution.py:24
  49.0 11.9 %collective-permute-start.7 = (bf16[64,1024]{1,0:T(8,128)(2,1)S(1)}, bf16[64,1024]{1,0:T(8,128)(2,1)S(1)}, u32[]{:S(2)}, u32[]{:S(2)}) collective-permute-start(bf16[64,1024]{1,0:T(8,128)(2,1)S(1)} %get-tuple-element.24), channel_id=1, source_target_pairs={{0,896},{32,928},{64,960},{96,992},{128,0},{160,32},{192,64},{224,... | collective-permute-start | bytes 393224 | tf_op jit(solution)/shard_map/ppermute | solution.py:24
  60.9 0.7 collective-permute-done.3
  61.6 1.9 collective-permute-start.4
  63.5 0.0 collective-permute-done.7
  63.5 16.3 %collective-permute-done.4 = bf16[64,1024]{1,0:T(8,128)(2,1)S(1)} collective-permute-done((bf16[64,1024]{1,0:T(8,128)(2,1)S(1)}, bf16[64,1024]{1,0:T(8,128)(2,1)S(1)}, u32[]{:S(2)}, u32[]{:S(2)}) %collective-permute-start.4) | collective-permute-done | bytes 131104 | tf_op jit(solution)/shard_map/ppermute | solution.py:24
  79.8 0.1 fusion.1
  79.9 1.9 collective-permute-start.5
  81.8 7.6 %collective-permute-start.8 = (bf16[64,1024]{1,0:T(8,128)(2,1)S(1)}, bf16[64,1024]{1,0:T(8,128)(2,1)S(1)}, u32[]{:S(2)}, u32[]{:S(2)}) collective-permute-start(bf16[64,1024]{1,0:T(8,128)(2,1)S(1)} %get-tuple-element.22), channel_id=1, source_target_pairs={{0,896},{32,928},{64,960},{96,992},{128,0},{160,32},{192,64},{224,... | collective-permute-start | bytes 393224 | tf_op jit(solution)/shard_map/ppermute | solution.py:24
  89.4 7.1 %collective-permute-done.5 = bf16[64,1024]{1,0:T(8,128)(2,1)S(1)} collective-permute-done((bf16[64,1024]{1,0:T(8,128)(2,1)S(1)}, bf16[64,1024]{1,0:T(8,128)(2,1)S(1)}, u32[]{:S(2)}, u32[]{:S(2)}) %collective-permute-start.5) | collective-permute-done | bytes 131104 | tf_op jit(solution)/shard_map/ppermute | solution.py:24
  96.5 0.0 collective-permute-done.8
  96.5 0.1 fusion
  96.6 2.8 %collective-permute-start.6 = (bf16[64,1024]{1,0:T(8,128)(2,1)S(1)}, bf16[64,1024]{1,0:T(8,128)(2,1)S(1)}, u32[]{:S(2)}, u32[]{:S(2)}) collective-permute-start(bf16[64,1024]{1,0:T(8,128)(2,1)S(1)} %get-tuple-element.21), channel_id=1, source_target_pairs={{0,128},{32,160},{64,192},{96,224},{128,256},{160,288},{192,320},{... | collective-permute-start | bytes 393224 | tf_op jit(solution)/shard_map/ppermute | solution.py:24
  99.4 6.4 %collective-permute-start.9 = (bf16[64,1024]{1,0:T(8,128)(2,1)S(1)}, bf16[64,1024]{1,0:T(8,128)(2,1)S(1)}, u32[]{:S(2)}, u32[]{:S(2)}) collective-permute-start(bf16[64,1024]{1,0:T(8,128)(2,1)S(1)} %get-tuple-element.20), channel_id=1, source_target_pairs={{0,896},{32,928},{64,960},{96,992},{128,0},{160,32},{192,64},{224,... | collective-permute-start | bytes 393224 | tf_op jit(solution)/shard_map/ppermute | solution.py:24
  105.8 0.0 copy-done.2
  105.8 0.1 bitcast_convert_fusion
  105.9 0.0 copy-start.5
  105.9 0.7 copy-done.5
  106.6 0.1 dynamic_slice.3
  106.6 0.1 select_reduce_fusion.1.chosen_ref
  106.7 4.0 %collective-permute-done.6.refs_1_ = bf16[64,1024]{1,0:T(8,128)(2,1)S(1)} collective-permute-done((bf16[64,1024]{1,0:T(8,128)(2,1)S(1)}, bf16[64,1024]{1,0:T(8,128)(2,1)S(1)}, u32[]{:S(2)}, u32[]{:S(2)}) %collective-permute-start.6) | collective-permute-done | bytes 131104 | tf_op jit(solution)/shard_map/ppermute | solution.py:24
  110.7 0.5 collective-permute-done.9.refs_2_
  111.3 1.5 shard_map.61
  112.8 10.2 %collective-permute-start.10 = (bf16[512,512]{1,0:T(8,128)(2,1)S(1)}, bf16[512,512]{1,0:T(8,128)(2,1)S(1)}, u32[]{:S(2)}, u32[]{:S(2)}) collective-permute-start(bf16[512,512]{1,0:T(8,128)(2,1)S(1)} %bitcast_convert_fusion), channel_id=1, source_target_pairs={{0,32},{32,0},{64,96},{96,64},{128,160},{160,128},{192,224},{224,1... | collective-permute-start | bytes 1572872 | tf_op jit(solution)/shard_map/ppermute | solution.py:17
  123.1 13.0 %all-to-all-start = ((bf16[32,64,128]{2,1,0:T(8,128)(2,1)}), bf16[32,64,128]{2,1,0:T(8,128)(2,1)S(1)}, u32[]{:S(2)}, u32[]{:S(2)}) async-start(bf16[32,64,128]{2,1,0:T(8,128)(2,1)} %shard_map.61), calls=%async_computation | async-start | bytes 1048576 | tf_op jit(solution)/shard_map/all_to_all | solution.py:283
  136.0 0.2 convert_reduce_fusion
  136.2 0.1 select_reduce_fusion.source_ref
  136.4 11.3 %all-to-all-done.incoming_ref = bf16[32,64,128]{2,1,0:T(8,128)(2,1)S(1)} async-done(((bf16[32,64,128]{2,1,0:T(8,128)(2,1)}), bf16[32,64,128]{2,1,0:T(8,128)(2,1)S(1)}, u32[]{:S(2)}, u32[]{:S(2)}) %all-to-all-start) | async-done | bytes 524320 | tf_op jit(solution)/shard_map/all_to_all | solution.py:283
  147.7 0.0 collective-permute-done.10.other_factor
  147.7 0.6 shard_map.62
  148.3 48.7 %all_to_all.10.own_half = bf16[16,64,128]{2,1,0:T(8,128)(2,1)S(1)} all-to-all(bf16[16,64,128]{2,1,0:T(8,128)(2,1)S(1)} %shard_map.62), channel_id=1, replica_groups={{0,64,128,192,256,320,384,448,512,576,640,704,768,832,896,960},{32,96,1..., dimensions={0} | all-to-all | bytes 524288 | tf_op jit(solution)/shard_map/all_to_all | solution.py:285
  197.0 1.9 collective-permute-start.11
  198.9 5.2 %collective-permute-done.11.other_half = bf16[16,64,128]{2,1,0:T(8,128)(2,1)S(1)} collective-permute-done((bf16[16,64,128]{2,1,0:T(8,128)(2,1)S(1)}, bf16[16,64,128]{2,1,0:T(8,128)(2,1)S(1)}, u32[]{:S(2)}, u32[]{:S(2)}) %collective-permute-start.11) | collective-permute-done | bytes 262176 | tf_op jit(solution)/shard_map/ppermute | solution.py:17
  204.1 5.1 %shard_map.63 = (f32[512,512]{1,0:T(8,128)}, bf16[256,512]{1,0:T(8,128)(2,1)}) custom-call(s32[1]{0:T(128)S(6)} %select_n.37.parity_ref, bf16[16,64,128]{2,1,0:T(8,128)(2,1)S(1)} %all_to_all.10.own_half, bf16[16,64,128]{2,1,0:T(8,128)(2,1)S(1)} %collective-permute-done.11.other_half, f32[512,512]{1,0:T(8,128)S(1)} %bitcast.36, ...), custom_call_target="tpu_custom_call" | custom-call | flops 2550136832 | bytes 3145728 | tf_op jit(solution)/shard_map/pallas_call | solution.py:83
  (7 shorter events, 0.1 us)
Async XLA Ops:
  0.6 1.2 copy-start
  1.9 0.9 copy-start.3
  2.8 34.4 %copy-start.1 = (bf16[128,4096]{1,0:T(8,128)(2,1)S(1)}, bf16[128,4096]{1,0:T(8,128)(2,1)}, u32[]{:S(2)}) copy-start(bf16[128,4096]{1,0:T(8,128)(2,1)} %grads_ref.3) | copy-start | bytes 3145732
  2.8 34.4 %copy-start.4 = (bf16[128,512]{1,0:T(8,128)(2,1)S(1)}, bf16[128,512]{1,0:T(8,128)(2,1)}, u32[]{:S(2)}) copy-start(bf16[128,512]{1,0:T(8,128)(2,1)} %acts_ref.3) | copy-start | bytes 393220
  3.0 30.9 %collective-permute-start = (bf16[128,1536]{1,0:T(8,128)(2,1)S(1)}, bf16[128,1536]{1,0:T(8,128)(2,1)S(1)}, u32[]{:S(2)}, u32[]{:S(2)}) collective-permute-start(bf16[128,1536]{1,0:T(8,128)(2,1)S(1)} %get-tuple-element.11), channel_id=1, source_target_pairs={{0,64},{32,96},{64,0},{96,32},{128,192},{160,224},{192,128},{224,1... | collective-permute-start | bytes 1179656 | tf_op jit(solution)/shard_map/ppermute | solution.py:17
  8.9 25.0 %collective-permute-start.1 = (bf16[128,1536]{1,0:T(8,128)(2,1)S(1)}, bf16[128,1536]{1,0:T(8,128)(2,1)S(1)}, u32[]{:S(2)}, u32[]{:S(2)}) collective-permute-start(bf16[128,1536]{1,0:T(8,128)(2,1)S(1)} %get-tuple-element.12), channel_id=1, source_target_pairs={{0,96},{32,64},{64,32},{96,0},{128,224},{160,192},{192,160},{224,1... | collective-permute-start | bytes 1179656 | tf_op jit(solution)/shard_map/ppermute | solution.py:17
  12.2 25.0 %collective-permute-start.2 = (bf16[128,1536]{1,0:T(8,128)(2,1)S(1)}, bf16[128,1536]{1,0:T(8,128)(2,1)S(1)}, u32[]{:S(2)}, u32[]{:S(2)}) collective-permute-start(bf16[128,1536]{1,0:T(8,128)(2,1)S(1)} %get-tuple-element.13), channel_id=1, source_target_pairs={{0,32},{32,0},{64,96},{96,64},{128,160},{160,128},{192,224},{224,1... | collective-permute-start | bytes 1179656 | tf_op jit(solution)/shard_map/ppermute | solution.py:17
  38.1 67.7 %copy-start.2 = (f32[1,1,512,512]{3,2,1,0:T(8,128)S(1)}, f32[1,1,512,512]{3,2,1,0:T(8,128)}, u32[]{:S(2)}) copy-start(f32[1,1,512,512]{3,2,1,0:T(8,128)} %param.7) | copy-start | bytes 3145732
  38.1 23.5 %collective-permute-start.3 = (bf16[64,1024]{1,0:T(8,128)(2,1)S(1)}, bf16[64,1024]{1,0:T(8,128)(2,1)S(1)}, u32[]{:S(2)}, u32[]{:S(2)}) collective-permute-start(bf16[64,1024]{1,0:T(8,128)(2,1)S(1)} %get-tuple-element.25), channel_id=1, source_target_pairs={{0,128},{32,160},{64,192},{96,224},{128,256},{160,288},{192,320},{... | collective-permute-start | bytes 393224 | tf_op jit(solution)/shard_map/ppermute | solution.py:24
  49.0 14.6 %collective-permute-start.7 = (bf16[64,1024]{1,0:T(8,128)(2,1)S(1)}, bf16[64,1024]{1,0:T(8,128)(2,1)S(1)}, u32[]{:S(2)}, u32[]{:S(2)}) collective-permute-start(bf16[64,1024]{1,0:T(8,128)(2,1)S(1)} %get-tuple-element.24), channel_id=1, source_target_pairs={{0,896},{32,928},{64,960},{96,992},{128,0},{160,32},{192,64},{224,... | collective-permute-start | bytes 393224 | tf_op jit(solution)/shard_map/ppermute | solution.py:24
  61.6 18.2 %collective-permute-start.4 = (bf16[64,1024]{1,0:T(8,128)(2,1)S(1)}, bf16[64,1024]{1,0:T(8,128)(2,1)S(1)}, u32[]{:S(2)}, u32[]{:S(2)}) collective-permute-start(bf16[64,1024]{1,0:T(8,128)(2,1)S(1)} %fusion.4), channel_id=1, source_target_pairs={{0,128},{32,160},{64,192},{96,224},{128,256},{160,288},{192,320},{... | collective-permute-start | bytes 393224 | tf_op jit(solution)/shard_map/ppermute | solution.py:24
  79.9 16.6 %collective-permute-start.5 = (bf16[64,1024]{1,0:T(8,128)(2,1)S(1)}, bf16[64,1024]{1,0:T(8,128)(2,1)S(1)}, u32[]{:S(2)}, u32[]{:S(2)}) collective-permute-start(bf16[64,1024]{1,0:T(8,128)(2,1)S(1)} %get-tuple-element.23), channel_id=1, source_target_pairs={{0,128},{32,160},{64,192},{96,224},{128,256},{160,288},{192,320},{... | collective-permute-start | bytes 393224 | tf_op jit(solution)/shard_map/ppermute | solution.py:24
  81.8 14.7 %collective-permute-start.8 = (bf16[64,1024]{1,0:T(8,128)(2,1)S(1)}, bf16[64,1024]{1,0:T(8,128)(2,1)S(1)}, u32[]{:S(2)}, u32[]{:S(2)}) collective-permute-start(bf16[64,1024]{1,0:T(8,128)(2,1)S(1)} %get-tuple-element.22), channel_id=1, source_target_pairs={{0,896},{32,928},{64,960},{96,992},{128,0},{160,32},{192,64},{224,... | collective-permute-start | bytes 393224 | tf_op jit(solution)/shard_map/ppermute | solution.py:24
  96.6 14.1 %collective-permute-start.6 = (bf16[64,1024]{1,0:T(8,128)(2,1)S(1)}, bf16[64,1024]{1,0:T(8,128)(2,1)S(1)}, u32[]{:S(2)}, u32[]{:S(2)}) collective-permute-start(bf16[64,1024]{1,0:T(8,128)(2,1)S(1)} %get-tuple-element.21), channel_id=1, source_target_pairs={{0,128},{32,160},{64,192},{96,224},{128,256},{160,288},{192,320},{... | collective-permute-start | bytes 393224 | tf_op jit(solution)/shard_map/ppermute | solution.py:24
  99.4 11.9 %collective-permute-start.9 = (bf16[64,1024]{1,0:T(8,128)(2,1)S(1)}, bf16[64,1024]{1,0:T(8,128)(2,1)S(1)}, u32[]{:S(2)}, u32[]{:S(2)}) collective-permute-start(bf16[64,1024]{1,0:T(8,128)(2,1)S(1)} %get-tuple-element.20), channel_id=1, source_target_pairs={{0,896},{32,928},{64,960},{96,992},{128,0},{160,32},{192,64},{224,... | collective-permute-start | bytes 393224 | tf_op jit(solution)/shard_map/ppermute | solution.py:24
  105.9 0.7 copy-start.5
  112.8 34.8 %collective-permute-start.10 = (bf16[512,512]{1,0:T(8,128)(2,1)S(1)}, bf16[512,512]{1,0:T(8,128)(2,1)S(1)}, u32[]{:S(2)}, u32[]{:S(2)}) collective-permute-start(bf16[512,512]{1,0:T(8,128)(2,1)S(1)} %bitcast_convert_fusion), channel_id=1, source_target_pairs={{0,32},{32,0},{64,96},{96,64},{128,160},{160,128},{192,224},{224,1... | collective-permute-start | bytes 1572872 | tf_op jit(solution)/shard_map/ppermute | solution.py:17
  123.1 24.6 %all-to-all-start = ((bf16[32,64,128]{2,1,0:T(8,128)(2,1)}), bf16[32,64,128]{2,1,0:T(8,128)(2,1)S(1)}, u32[]{:S(2)}, u32[]{:S(2)}) async-start(bf16[32,64,128]{2,1,0:T(8,128)(2,1)} %shard_map.61), calls=%async_computation | async-start | bytes 1048576 | tf_op jit(solution)/shard_map/all_to_all | solution.py:283
  197.0 7.1 %collective-permute-start.11 = (bf16[16,64,128]{2,1,0:T(8,128)(2,1)S(1)}, bf16[16,64,128]{2,1,0:T(8,128)(2,1)S(1)}, u32[]{:S(2)}, u32[]{:S(2)}) collective-permute-start(bf16[16,64,128]{2,1,0:T(8,128)(2,1)S(1)} %all_to_all.10.own_half), channel_id=1, source_target_pairs={{0,32},{32,0},{64,96},{96,64},{128,160},{160,128},{192,224},{224,1... | collective-permute-start | bytes 786440 | tf_op jit(solution)/shard_map/ppermute | solution.py:17

commit v3 on v2

--- a/solution.py
+++ b/solution.py
@@ -121,20 +121,24 @@
     width = block_width // team
     for mask, sent_ref in zip((2, 3, 1), sent_refs):
         quarter = quarter_of(member_ref[0] ^ mask)
-        sent_ref[:, :block_width] = acts_ref[...]
+        start = 0
+        if mask != 3:
+            start = block_width
+            sent_ref[:, :block_width] = acts_ref[...]
         for block in range(grads_ref.shape[1] // block_width):
-            at = block_width + block * width
+            at = start + block * width
             sent_ref[:, at : at + width] = grads_ref[:, wide(team * block + quarter, width)]
 
 
 def team_messages(member, acts, grads_out):
     tokens, block_width = acts.shape
-    message = jax.ShapeDtypeStruct(
-        (tokens, block_width + grads_out.shape[1] // team), acts.dtype
-    )
+    columns = grads_out.shape[1] // team
     return pl.pallas_call(
         send_kernel,
-        out_shape=(message,) * 3,
+        out_shape=tuple(
+            jax.ShapeDtypeStruct((tokens, extra + columns), acts.dtype)
+            for extra in (block_width, 0, block_width)
+        ),
         in_specs=[in_smem(), in_vmem(), in_vmem()],
         out_specs=(in_vmem(),) * 3,
         compiler_params=pltpu.CompilerParams(vmem_limit_bytes=24 * 2**20),
@@ -142,14 +146,13 @@
 
 
 def gradient_kernel(
-    member_ref, place_ref, acts_ref, grads_ref, first, second, third, partial_ref, whole
+    member_ref, place_ref, acts_ref, grads_ref, first, second, third, relayed, partial_ref, whole
 ):
     block_width = acts_ref.shape[1]
     width = block_width // team
-    messages = (first, second, third)
     quarter = quarter_of(member_ref[0])
     inputs = jnp.concatenate(
-        [acts_ref[...]] + [message[:, :block_width] for message in messages], axis=0
+        [acts_ref[...], first[:, :block_width], relayed[...], third[:, :block_width]], axis=0
     )
     blocks = grads_ref.shape[1] // block_width
     for pair in range(0, blocks, 2):
@@ -157,9 +160,15 @@
             [grads_ref[:, wide(team * block + quarter, width)] for block in (pair, pair + 1)],
             axis=1,
         )
-        at = block_width + pair * width
+        at, after = pair * width, block_width + pair * width
         cotangents = jnp.concatenate(
-            [own] + [message[:, at : at + 2 * width] for message in messages], axis=0
+            [
+                own,
+                first[:, after : after + 2 * width],
+                second[:, at : at + 2 * width],
+                third[:, after : after + 2 * width],
+            ],
+            axis=0,
         )
         whole[:, pair * width : (pair + 2) * width] = product(
             inputs, cotangents, ((0,), (0,))
@@ -176,7 +185,7 @@
     return pl.pallas_call(
         gradient_kernel,
         out_shape=jax.ShapeDtypeStruct((stops, block_width // stops, columns), jnp.bfloat16),
-        in_specs=[in_smem()] * 2 + [in_vmem()] * 5,
+        in_specs=[in_smem()] * 2 + [in_vmem()] * 6,
         out_specs=in_vmem(),
         scratch_shapes=[pltpu.VMEM((block_width, columns), jnp.bfloat16)],
         compiler_params=pltpu.CompilerParams(vmem_limit_bytes=32 * 2**20),
@@ -193,16 +202,18 @@
 
 
 def ring_terms(partial):
-    stops = partial.shape[0]
+    stops, _, columns = partial.shape
+    length = stops // 2 - 1
+    far = partial[length + 1]
     terms = [partial[0]]
-    for step, length in ((1, stops // 2), (-1, stops - 1 - stops // 2)):
-        if length:
-            chain = partial[step * length % stops]
-            for left in range(length - 1, -1, -1):
-                chain = along(chain, step * team)
-                if left:
-                    chain = plus(chain, partial[step * left % stops])
-            terms.append(chain)
+    for step, part in ((1, slice(0, columns // 2)), (-1, slice(columns // 2, columns))):
+        chain = partial[step * length % stops]
+        chain = chain.at[:, part].set(plus(chain[:, part], along(far[:, part], step * team)))
+        for left in range(length - 1, -1, -1):
+            chain = along(chain, step * team)
+            if left:
+                chain = plus(chain, partial[step * left % stops])
+        terms.append(chain)
     return terms
 
 
@@ -272,14 +283,13 @@
     placing = (slot_ids[:, None] == slot_of[None, :]) & (owner_of == grp_where)[None, :]
     source = jnp.max(jnp.where(placing, block_ids[None, :] // per_group, -1), axis=1)
 
+    own_factor = factors[0, 0]
+    other_factor = across(own_factor.astype(jnp.bfloat16), 1)
     sent = team_messages(member, acts, grads_out)
     messages = [across(message, mask) for mask, message in zip((2, 3, 1), sent)]
+    messages.append(across(messages[0][:, :block_width], 1))
     terms = ring_terms(team_gradient(member, place, stops, acts, grads_out, messages))
-    own_factor = factors[0, 0]
-    outgoing, factor_low = lax.optimization_barrier(
-        (by_owner(chosen, terms, block_width // team), own_factor.astype(jnp.bfloat16))
-    )
-    other_factor = across(factor_low, 1)
+    outgoing = by_owner(chosen, terms, block_width // team)
     incoming = lax.all_to_all(outgoing, "grp", split_axis=0, concat_axis=0, tiled=True)
     incoming, other_factor = lax.optimization_barrier((incoming, other_factor))
     own_half = lax.all_to_all(

time: 213 us -> 211 us (level); the launches traced: 209 us -> 210 us
  waiting for transfers between devices: 67.9 us -> 36 us
  starting transfers between devices: 79.9 us -> 110 us
    ppermute x7 -> x8, waiting for transfers between devices: 28.6 us -> 4.76 us  [along(): lax.ppermute(block, 'dp', [(place, (place + distance) % count) for place...]
    all_to_all x1, starting transfers between devices: 13 us -> 24.5 us  [per_device(): lax.all_to_all(outgoing, 'grp', split_axis=0, concat_axis=0, tiled=True)]
    ppermute x7 -> x8, starting transfers between devices: 43.4 us -> 54.7 us  [along(): lax.ppermute(block, 'dp', [(place, (place + distance) % count) for place...]
    ppermute x5 -> x6, waiting for transfers between devices: 28 us -> 20 us  [across(): lax.ppermute(block, 'dp', [(place, place ^ mask) for place in range(lax.a...]
    ppermute x5 -> x6, starting transfers between devices: 23.5 us -> 30.6 us  [across(): lax.ppermute(block, 'dp', [(place, place ^ mask) for place in range(lax.a...]
  transfers between devices with their start and end apart: 13 -> 15, of which waited for: 9 -> 8; matrix products, arithmetic and copies ran while one was open for 0% -> 1% of each run, Pallas kernels for 0% -> 1%
where the time goes in v3:
time: 211 us; the launch traced here: 210 us
  starting transfers between devices  110 us (52%)
  blocking collectives  50.1 us (24%)
  waiting for transfers between devices  36 us (17%)
  Pallas kernels  8.31 us (4%)
  local copies, waits for them, and re-layouts  2.94 us (1%)
    ppermute x8, starting transfers between devices, along(): lax.ppermute(block, 'dp', [(place, (place + distance) % count) for place...  54.7 us
    all_to_all x1, blocking collectives, per_device(): lax.all_to_all(by_slot(source, incoming), 'dp', split_axis=0, concat_axis...  50.1 us
    ppermute x6, starting transfers between devices, across(): lax.ppermute(block, 'dp', [(place, place ^ mask) for place in range(lax.a...  30.6 us
    all_to_all x1, starting transfers between devices, per_device(): lax.all_to_all(outgoing, 'grp', split_axis=0, concat_axis=0, tiled=True)  24.5 us
    ppermute x6, waiting for transfers between devices, across(): lax.ppermute(block, 'dp', [(place, place ^ mask) for place in range(lax.a...  20 us
    all_to_all x1, waiting for transfers between devices, per_device(): lax.all_to_all(outgoing, 'grp', split_axis=0, concat_axis=0, tiled=True)  11.3 us
    pallas_call x1, Pallas kernels, precondition(): pl.pallas_call(precondition_kernel, out_shape=(jax.ShapeDtypeStruct((size...  5.11 us
    ppermute x8, waiting for transfers between devices, along(): lax.ppermute(block, 'dp', [(place, (place + distance) % count) for place...  4.76 us
  transfers between devices with their start and end apart: 15, of which 8 were waited for; matrix products, arithmetic and copies ran while one was open for 1% of the time, Pallas kernels for 1%

profile of v3, /device:TPU:1, one launch (start us, length us, event | category | flops | bytes accessed | tf_op | source)
XLA Modules:
  0.0 210.2 jit_solution(809804456314112870)
XLA Ops:
  0.7 1.2 copy-done
  1.9 0.9 copy-done.3
  2.8 0.2 shard_map.59
  3.0 5.9 %collective-permute-start = (bf16[128,1536]{1,0:T(8,128)(2,1)S(1)}, bf16[128,1536]{1,0:T(8,128)(2,1)S(1)}, u32[]{:S(2)}, u32[]{:S(2)}) collective-permute-start(bf16[128,1536]{1,0:T(8,128)(2,1)S(1)} %get-tuple-element.33), channel_id=1, source_target_pairs={{0,64},{32,96},{64,0},{96,32},{128,192},{160,224},{192,128},{224,1... | collective-permute-start | bytes 1179656 | tf_op jit(solution)/shard_map/ppermute | solution.py:17
  8.9 3.5 %collective-permute-start.2 = (bf16[128,1536]{1,0:T(8,128)(2,1)S(1)}, bf16[128,1536]{1,0:T(8,128)(2,1)S(1)}, u32[]{:S(2)}, u32[]{:S(2)}) collective-permute-start(bf16[128,1536]{1,0:T(8,128)(2,1)S(1)} %get-tuple-element.35), channel_id=1, source_target_pairs={{0,32},{32,0},{64,96},{96,64},{128,160},{160,128},{192,224},{224,1... | collective-permute-start | bytes 1179656 | tf_op jit(solution)/shard_map/ppermute | solution.py:17
  12.4 0.0 copy-start.4
  12.4 2.1 collective-permute-start.1
  14.5 8.0 %collective-permute-done.first = bf16[128,1536]{1,0:T(8,128)(2,1)S(1)} collective-permute-done((bf16[128,1536]{1,0:T(8,128)(2,1)S(1)}, bf16[128,1536]{1,0:T(8,128)(2,1)S(1)}, u32[]{:S(2)}, u32[]{:S(2)}) %collective-permute-start) | collective-permute-done | bytes 393248 | tf_op jit(solution)/shard_map/ppermute | solution.py:17
  22.5 9.7 %collective-permute-start.3 = (bf16[128,512]{1,0:T(8,128)(2,1)S(1)}, bf16[128,512]{1,0:T(8,128)(2,1)S(1)}, u32[]{:S(2)}, u32[]{:S(2)}) collective-permute-start(bf16[128,512]{1,0:T(8,128)(2,1)S(1)} %slice.91), channel_id=1, source_target_pairs={{0,32},{32,0},{64,96},{96,64},{128,160},{160,128},{192,224},{224,1... | collective-permute-start | bytes 393224 | tf_op jit(solution)/shard_map/ppermute | solution.py:17
  32.1 0.0 collective-permute-done.1.second
  32.1 0.0 collective-permute-done.2.third
  32.2 6.2 %collective-permute-done.3.relayed = bf16[128,512]{1,0:T(8,128)(2,1)S(1)} collective-permute-done((bf16[128,512]{1,0:T(8,128)(2,1)S(1)}, bf16[128,512]{1,0:T(8,128)(2,1)S(1)}, u32[]{:S(2)}, u32[]{:S(2)}) %collective-permute-start.3) | collective-permute-done | bytes 131104 | tf_op jit(solution)/shard_map/ppermute | solution.py:17
  38.4 0.8 shard_map.60
  39.3 0.0 copy-start.2
  39.3 7.6 %collective-permute-start.4 = (bf16[64,512]{1,0:T(8,128)(2,1)S(1)}, bf16[64,512]{1,0:T(8,128)(2,1)S(1)}, u32[]{:S(2)}, u32[]{:S(2)}) collective-permute-start(bf16[64,512]{1,0:T(8,128)(2,1)S(1)} %get-tuple-element.49), channel_id=1, source_target_pairs={{0,128},{32,160},{64,192},{96,224},{128,256},{160,288},{192,320},{... | collective-permute-start | bytes 196616 | tf_op jit(solution)/shard_map/ppermute | solution.py:24
  46.9 0.6 compare_reduce_fusion
  47.5 10.5 %collective-permute-start.8 = (bf16[64,512]{1,0:T(8,128)(2,1)S(1)}, bf16[64,512]{1,0:T(8,128)(2,1)S(1)}, u32[]{:S(2)}, u32[]{:S(2)}) collective-permute-start(bf16[64,512]{1,0:T(8,128)(2,1)S(1)} %get-tuple-element.48), channel_id=1, source_target_pairs={{0,896},{32,928},{64,960},{96,992},{128,0},{160,32},{192,64},{224,... | collective-permute-start | bytes 196616 | tf_op jit(solution)/shard_map/ppermute | solution.py:24
  58.1 0.0 collective-permute-done.4
  58.1 0.7 fusion.6
  58.8 1.9 collective-permute-start.5
  60.7 7.3 %collective-permute-start.9 = (bf16[64,1024]{1,0:T(8,128)(2,1)S(1)}, bf16[64,1024]{1,0:T(8,128)(2,1)S(1)}, u32[]{:S(2)}, u32[]{:S(2)}) collective-permute-start(bf16[64,1024]{1,0:T(8,128)(2,1)S(1)} %fusion.7), channel_id=1, source_target_pairs={{0,896},{32,928},{64,960},{96,992},{128,0},{160,32},{192,64},{224,... | collective-permute-start | bytes 393224 | tf_op jit(solution)/shard_map/ppermute | solution.py:24
  68.0 0.8 collective-permute-done.5
  68.8 2.0 collective-permute-done.9
  70.8 0.1 fusion.1
  70.9 6.8 %collective-permute-start.10 = (bf16[64,1024]{1,0:T(8,128)(2,1)S(1)}, bf16[64,1024]{1,0:T(8,128)(2,1)S(1)}, u32[]{:S(2)}, u32[]{:S(2)}) collective-permute-start(bf16[64,1024]{1,0:T(8,128)(2,1)S(1)} %get-tuple-element.42), channel_id=1, source_target_pairs={{0,896},{32,928},{64,960},{96,992},{128,0},{160,32},{192,64},{224,... | collective-permute-start | bytes 393224 | tf_op jit(solution)/shard_map/ppermute | solution.py:24
  77.7 10.8 %collective-permute-start.6 = (bf16[64,1024]{1,0:T(8,128)(2,1)S(1)}, bf16[64,1024]{1,0:T(8,128)(2,1)S(1)}, u32[]{:S(2)}, u32[]{:S(2)}) collective-permute-start(bf16[64,1024]{1,0:T(8,128)(2,1)S(1)} %get-tuple-element.43), channel_id=1, source_target_pairs={{0,128},{32,160},{64,192},{96,224},{128,256},{160,288},{192,320},{... | collective-permute-start | bytes 393224 | tf_op jit(solution)/shard_map/ppermute | solution.py:24
  88.5 1.3 collective-permute-done.10
  89.8 0.6 collective-permute-done.6
  90.4 0.1 fusion
  90.5 4.3 %collective-permute-start.11 = (bf16[64,1024]{1,0:T(8,128)(2,1)S(1)}, bf16[64,1024]{1,0:T(8,128)(2,1)S(1)}, u32[]{:S(2)}, u32[]{:S(2)}) collective-permute-start(bf16[64,1024]{1,0:T(8,128)(2,1)S(1)} %get-tuple-element.40), channel_id=1, source_target_pairs={{0,896},{32,928},{64,960},{96,992},{128,0},{160,32},{192,64},{224,... | collective-permute-start | bytes 393224 | tf_op jit(solution)/shard_map/ppermute | solution.py:24
  94.8 5.5 %collective-permute-start.7 = (bf16[64,1024]{1,0:T(8,128)(2,1)S(1)}, bf16[64,1024]{1,0:T(8,128)(2,1)S(1)}, u32[]{:S(2)}, u32[]{:S(2)}) collective-permute-start(bf16[64,1024]{1,0:T(8,128)(2,1)S(1)} %get-tuple-element.41), channel_id=1, source_target_pairs={{0,128},{32,160},{64,192},{96,224},{128,256},{160,288},{192,320},{... | collective-permute-start | bytes 393224 | tf_op jit(solution)/shard_map/ppermute | solution.py:24
  100.3 0.1 bitcast_convert_fusion
  100.4 7.6 %collective-permute-start.12 = (bf16[512,512]{1,0:T(8,128)(2,1)S(1)}, bf16[512,512]{1,0:T(8,128)(2,1)S(1)}, u32[]{:S(2)}, u32[]{:S(2)}) collective-permute-start(bf16[512,512]{1,0:T(8,128)(2,1)S(1)} %bitcast_convert_fusion), channel_id=1, source_target_pairs={{0,32},{32,0},{64,96},{96,64},{128,160},{160,128},{192,224},{224,1... | collective-permute-start | bytes 1572872 | tf_op jit(solution)/shard_map/ppermute | solution.py:17
  108.0 0.0 copy-start.5
  108.0 0.7 copy-done.5
  108.7 0.1 dynamic_slice.3
  108.8 0.1 select_reduce_fusion.1.chosen_ref
  108.9 1.5 shard_map.61
  110.4 24.5 %all-to-all-start = ((bf16[32,64,128]{2,1,0:T(8,128)(2,1)}), bf16[32,64,128]{2,1,0:T(8,128)(2,1)S(1)}, u32[]{:S(2)}, u32[]{:S(2)}) async-start(bf16[32,64,128]{2,1,0:T(8,128)(2,1)} %shard_map.61), calls=%async_computation | async-start | bytes 1048576 | tf_op jit(solution)/shard_map/all_to_all | solution.py:293
  135.0 0.2 convert_reduce_fusion
  135.1 0.1 select_reduce_fusion.source_ref
  135.3 0.0 collective-permute-done.12.other_factor
  135.3 11.3 %all-to-all-done.incoming_ref = bf16[32,64,128]{2,1,0:T(8,128)(2,1)S(1)} async-done(((bf16[32,64,128]{2,1,0:T(8,128)(2,1)}), bf16[32,64,128]{2,1,0:T(8,128)(2,1)S(1)}, u32[]{:S(2)}, u32[]{:S(2)}) %all-to-all-start) | async-done | bytes 524320 | tf_op jit(solution)/shard_map/all_to_all | solution.py:293
  146.6 0.6 shard_map.62
  147.2 50.1 %all_to_all.10.own_half = bf16[16,64,128]{2,1,0:T(8,128)(2,1)S(1)} all-to-all(bf16[16,64,128]{2,1,0:T(8,128)(2,1)S(1)} %shard_map.62), channel_id=1, replica_groups={{0,64,128,192,256,320,384,448,512,576,640,704,768,832,896,960},{32,96,1..., dimensions={0} | all-to-all | bytes 524288 | tf_op jit(solution)/shard_map/all_to_all | solution.py:295
  197.3 1.9 collective-permute-start.13
  199.3 5.8 %collective-permute-done.13.other_half = bf16[16,64,128]{2,1,0:T(8,128)(2,1)S(1)} collective-permute-done((bf16[16,64,128]{2,1,0:T(8,128)(2,1)S(1)}, bf16[16,64,128]{2,1,0:T(8,128)(2,1)S(1)}, u32[]{:S(2)}, u32[]{:S(2)}) %collective-permute-start.13) | collective-permute-done | bytes 262176 | tf_op jit(solution)/shard_map/ppermute | solution.py:17
  205.1 5.1 %shard_map.63 = (f32[512,512]{1,0:T(8,128)}, bf16[256,512]{1,0:T(8,128)(2,1)}) custom-call(s32[1]{0:T(128)S(6)} %select_n.37.parity_ref, bf16[16,64,128]{2,1,0:T(8,128)(2,1)S(1)} %all_to_all.10.own_half, bf16[16,64,128]{2,1,0:T(8,128)(2,1)S(1)} %collective-permute-done.13.other_half, f32[512,512]{1,0:T(8,128)S(1)} %bitcast.37, ...), custom_call_target="tpu_custom_call" | custom-call | flops 2550136832 | bytes 3145728 | tf_op jit(solution)/shard_map/pallas_call | solution.py:83
  (15 shorter events, 0.1 us)
Async XLA Ops:
  0.6 1.2 copy-start
  1.9 0.9 copy-start.3
  2.8 35.6 %copy-start.1 = (bf16[128,4096]{1,0:T(8,128)(2,1)S(1)}, bf16[128,4096]{1,0:T(8,128)(2,1)}, u32[]{:S(2)}) copy-start(bf16[128,4096]{1,0:T(8,128)(2,1)} %grads_ref.3) | copy-start | bytes 3145732
  3.0 19.4 %collective-permute-start = (bf16[128,1536]{1,0:T(8,128)(2,1)S(1)}, bf16[128,1536]{1,0:T(8,128)(2,1)S(1)}, u32[]{:S(2)}, u32[]{:S(2)}) collective-permute-start(bf16[128,1536]{1,0:T(8,128)(2,1)S(1)} %get-tuple-element.33), channel_id=1, source_target_pairs={{0,64},{32,96},{64,0},{96,32},{128,192},{160,224},{192,128},{224,1... | collective-permute-start | bytes 1179656 | tf_op jit(solution)/shard_map/ppermute | solution.py:17
  8.9 23.3 %collective-permute-start.2 = (bf16[128,1536]{1,0:T(8,128)(2,1)S(1)}, bf16[128,1536]{1,0:T(8,128)(2,1)S(1)}, u32[]{:S(2)}, u32[]{:S(2)}) collective-permute-start(bf16[128,1536]{1,0:T(8,128)(2,1)S(1)} %get-tuple-element.35), channel_id=1, source_target_pairs={{0,32},{32,0},{64,96},{96,64},{128,160},{160,128},{192,224},{224,1... | collective-permute-start | bytes 1179656 | tf_op jit(solution)/shard_map/ppermute | solution.py:17
  12.4 25.9 %copy-start.4 = (bf16[128,512]{1,0:T(8,128)(2,1)S(1)}, bf16[128,512]{1,0:T(8,128)(2,1)}, u32[]{:S(2)}) copy-start(bf16[128,512]{1,0:T(8,128)(2,1)} %acts_ref.3) | copy-start | bytes 393220
  12.4 19.7 %collective-permute-start.1 = (bf16[128,1024]{1,0:T(8,128)(2,1)S(1)}, bf16[128,1024]{1,0:T(8,128)(2,1)S(1)}, u32[]{:S(2)}, u32[]{:S(2)}) collective-permute-start(bf16[128,1024]{1,0:T(8,128)(2,1)S(1)} %get-tuple-element.34), channel_id=1, source_target_pairs={{0,96},{32,64},{64,32},{96,0},{128,224},{160,192},{192,160},{224,1... | collective-permute-start | bytes 786440 | tf_op jit(solution)/shard_map/ppermute | solution.py:17
  22.5 15.9 %collective-permute-start.3 = (bf16[128,512]{1,0:T(8,128)(2,1)S(1)}, bf16[128,512]{1,0:T(8,128)(2,1)S(1)}, u32[]{:S(2)}, u32[]{:S(2)}) collective-permute-start(bf16[128,512]{1,0:T(8,128)(2,1)S(1)} %slice.91), channel_id=1, source_target_pairs={{0,32},{32,0},{64,96},{96,64},{128,160},{160,128},{192,224},{224,1... | collective-permute-start | bytes 393224 | tf_op jit(solution)/shard_map/ppermute | solution.py:17
  39.3 61.1 %copy-start.2 = (f32[1,1,512,512]{3,2,1,0:T(8,128)S(1)}, f32[1,1,512,512]{3,2,1,0:T(8,128)}, u32[]{:S(2)}) copy-start(f32[1,1,512,512]{3,2,1,0:T(8,128)} %param.11) | copy-start | bytes 3145732
  39.3 18.8 %collective-permute-start.4 = (bf16[64,512]{1,0:T(8,128)(2,1)S(1)}, bf16[64,512]{1,0:T(8,128)(2,1)S(1)}, u32[]{:S(2)}, u32[]{:S(2)}) collective-permute-start(bf16[64,512]{1,0:T(8,128)(2,1)S(1)} %get-tuple-element.49), channel_id=1, source_target_pairs={{0,128},{32,160},{64,192},{96,224},{128,256},{160,288},{192,320},{... | collective-permute-start | bytes 196616 | tf_op jit(solution)/shard_map/ppermute | solution.py:24
  47.5 13.2 %collective-permute-start.8 = (bf16[64,512]{1,0:T(8,128)(2,1)S(1)}, bf16[64,512]{1,0:T(8,128)(2,1)S(1)}, u32[]{:S(2)}, u32[]{:S(2)}) collective-permute-start(bf16[64,512]{1,0:T(8,128)(2,1)S(1)} %get-tuple-element.48), channel_id=1, source_target_pairs={{0,896},{32,928},{64,960},{96,992},{128,0},{160,32},{192,64},{224,... | collective-permute-start | bytes 196616 | tf_op jit(solution)/shard_map/ppermute | solution.py:24
  58.8 10.1 %collective-permute-start.5 = (bf16[64,1024]{1,0:T(8,128)(2,1)S(1)}, bf16[64,1024]{1,0:T(8,128)(2,1)S(1)}, u32[]{:S(2)}, u32[]{:S(2)}) collective-permute-start(bf16[64,1024]{1,0:T(8,128)(2,1)S(1)} %fusion.6), channel_id=1, source_target_pairs={{0,128},{32,160},{64,192},{96,224},{128,256},{160,288},{192,320},{... | collective-permute-start | bytes 393224 | tf_op jit(solution)/shard_map/ppermute | solution.py:24
  60.7 10.1 %collective-permute-start.9 = (bf16[64,1024]{1,0:T(8,128)(2,1)S(1)}, bf16[64,1024]{1,0:T(8,128)(2,1)S(1)}, u32[]{:S(2)}, u32[]{:S(2)}) collective-permute-start(bf16[64,1024]{1,0:T(8,128)(2,1)S(1)} %fusion.7), channel_id=1, source_target_pairs={{0,896},{32,928},{64,960},{96,992},{128,0},{160,32},{192,64},{224,... | collective-permute-start | bytes 393224 | tf_op jit(solution)/shard_map/ppermute | solution.py:24
  70.9 19.0 %collective-permute-start.10 = (bf16[64,1024]{1,0:T(8,128)(2,1)S(1)}, bf16[64,1024]{1,0:T(8,128)(2,1)S(1)}, u32[]{:S(2)}, u32[]{:S(2)}) collective-permute-start(bf16[64,1024]{1,0:T(8,128)(2,1)S(1)} %get-tuple-element.42), channel_id=1, source_target_pairs={{0,896},{32,928},{64,960},{96,992},{128,0},{160,32},{192,64},{224,... | collective-permute-start | bytes 393224 | tf_op jit(solution)/shard_map/ppermute | solution.py:24
  77.7 12.7 %collective-permute-start.6 = (bf16[64,1024]{1,0:T(8,128)(2,1)S(1)}, bf16[64,1024]{1,0:T(8,128)(2,1)S(1)}, u32[]{:S(2)}, u32[]{:S(2)}) collective-permute-start(bf16[64,1024]{1,0:T(8,128)(2,1)S(1)} %get-tuple-element.43), channel_id=1, source_target_pairs={{0,128},{32,160},{64,192},{96,224},{128,256},{160,288},{192,320},{... | collective-permute-start | bytes 393224 | tf_op jit(solution)/shard_map/ppermute | solution.py:24
  90.5 18.3 %collective-permute-start.11 = (bf16[64,1024]{1,0:T(8,128)(2,1)S(1)}, bf16[64,1024]{1,0:T(8,128)(2,1)S(1)}, u32[]{:S(2)}, u32[]{:S(2)}) collective-permute-start(bf16[64,1024]{1,0:T(8,128)(2,1)S(1)} %get-tuple-element.40), channel_id=1, source_target_pairs={{0,896},{32,928},{64,960},{96,992},{128,0},{160,32},{192,64},{224,... | collective-permute-start | bytes 393224 | tf_op jit(solution)/shard_map/ppermute | solution.py:24
  94.8 14.0 %collective-permute-start.7 = (bf16[64,1024]{1,0:T(8,128)(2,1)S(1)}, bf16[64,1024]{1,0:T(8,128)(2,1)S(1)}, u32[]{:S(2)}, u32[]{:S(2)}) collective-permute-start(bf16[64,1024]{1,0:T(8,128)(2,1)S(1)} %get-tuple-element.41), channel_id=1, source_target_pairs={{0,128},{32,160},{64,192},{96,224},{128,256},{160,288},{192,320},{... | collective-permute-start | bytes 393224 | tf_op jit(solution)/shard_map/ppermute | solution.py:24
  100.4 34.9 %collective-permute-start.12 = (bf16[512,512]{1,0:T(8,128)(2,1)S(1)}, bf16[512,512]{1,0:T(8,128)(2,1)S(1)}, u32[]{:S(2)}, u32[]{:S(2)}) collective-permute-start(bf16[512,512]{1,0:T(8,128)(2,1)S(1)} %bitcast_convert_fusion), channel_id=1, source_target_pairs={{0,32},{32,0},{64,96},{96,64},{128,160},{160,128},{192,224},{224,1... | collective-permute-start | bytes 1572872 | tf_op jit(solution)/shard_map/ppermute | solution.py:17
  108.0 0.7 copy-start.5
  110.4 36.2 %all-to-all-start = ((bf16[32,64,128]{2,1,0:T(8,128)(2,1)}), bf16[32,64,128]{2,1,0:T(8,128)(2,1)S(1)}, u32[]{:S(2)}, u32[]{:S(2)}) async-start(bf16[32,64,128]{2,1,0:T(8,128)(2,1)} %shard_map.61), calls=%async_computation | async-start | bytes 1048576 | tf_op jit(solution)/shard_map/all_to_all | solution.py:293
  197.3 7.7 %collective-permute-start.13 = (bf16[16,64,128]{2,1,0:T(8,128)(2,1)S(1)}, bf16[16,64,128]{2,1,0:T(8,128)(2,1)S(1)}, u32[]{:S(2)}, u32[]{:S(2)}) collective-permute-start(bf16[16,64,128]{2,1,0:T(8,128)(2,1)S(1)} %all_to_all.10.own_half), channel_id=1, source_target_pairs={{0,32},{32,0},{64,96},{96,64},{128,160},{160,128},{192,224},{224,1... | collective-permute-start | bytes 786440 | tf_op jit(solution)/shard_map/ppermute | solution.py:17

commit v4 on v3

--- a/solution.py
+++ b/solution.py
@@ -202,13 +202,13 @@
 
 
 def ring_terms(partial):
-    stops, _, columns = partial.shape
+    stops, rows, _ = partial.shape
     length = stops // 2 - 1
     far = partial[length + 1]
     terms = [partial[0]]
-    for step, part in ((1, slice(0, columns // 2)), (-1, slice(columns // 2, columns))):
+    for step, part in ((1, slice(0, rows // 2)), (-1, slice(rows // 2, rows))):
         chain = partial[step * length % stops]
-        chain = chain.at[:, part].set(plus(chain[:, part], along(far[:, part], step * team)))
+        chain = chain.at[part].set(plus(chain[part], along(far[part], step * team)))
         for left in range(length - 1, -1, -1):
             chain = along(chain, step * team)
             if left:

time: 211 us -> 211 us (level); the launches traced: 210 us -> 207 us
  blocking collectives: 50.1 us -> 37 us
  waiting for transfers between devices: 36 us -> 42.7 us
  starting transfers between devices: 110 us -> 115 us
    ppermute x6, starting transfers between devices: 30.6 us -> 47 us  [across(): lax.ppermute(block, 'dp', [(place, place ^ mask) for place in range(lax.a...]
    all_to_all x1, blocking collectives: 50.1 us -> 37 us  [per_device(): lax.all_to_all(by_slot(source, incoming), 'dp', split_axis=0, concat_axis...]
    ppermute x8, starting transfers between devices: 54.7 us -> 45.9 us  [along(): lax.ppermute(block, 'dp', [(place, (place + distance) % count) for place...]
    ppermute x8, waiting for transfers between devices: 4.76 us -> 13.6 us  [along(): lax.ppermute(block, 'dp', [(place, (place + distance) % count) for place...]
    all_to_all x1, starting transfers between devices: 24.5 us -> 21.7 us  [per_device(): lax.all_to_all(outgoing, 'grp', split_axis=0, concat_axis=0, tiled=True)]
  transfers between devices with their start and end apart: 15 -> 15, of which waited for: 8 -> 8; matrix products, arithmetic and copies ran while one was open for 1% -> 0% of each run, Pallas kernels for 1% -> 1%
where the time goes in v4:
time: 211 us; the launch traced here: 207 us
  starting transfers between devices  115 us (55%)
  waiting for transfers between devices  42.7 us (20%)
  blocking collectives  37 us (18%)
  Pallas kernels  8.32 us (4%)
  local copies, waits for them, and re-layouts  2.93 us (1%)
    ppermute x6, starting transfers between devices, across(): lax.ppermute(block, 'dp', [(place, place ^ mask) for place in range(lax.a...  47 us
    ppermute x8, starting transfers between devices, along(): lax.ppermute(block, 'dp', [(place, (place + distance) % count) for place...  45.9 us
    all_to_all x1, blocking collectives, per_device(): lax.all_to_all(by_slot(source, incoming), 'dp', split_axis=0, concat_axis...  37 us
    all_to_all x1, starting transfers between devices, per_device(): lax.all_to_all(outgoing, 'grp', split_axis=0, concat_axis=0, tiled=True)  21.7 us
    ppermute x6, waiting for transfers between devices, across(): lax.ppermute(block, 'dp', [(place, place ^ mask) for place in range(lax.a...  17.9 us
    ppermute x8, waiting for transfers between devices, along(): lax.ppermute(block, 'dp', [(place, (place + distance) % count) for place...  13.6 us
    all_to_all x1, waiting for transfers between devices, per_device(): lax.all_to_all(outgoing, 'grp', split_axis=0, concat_axis=0, tiled=True)  11.3 us
    pallas_call x1, Pallas kernels, precondition(): pl.pallas_call(precondition_kernel, out_shape=(jax.ShapeDtypeStruct((size...  5.12 us
  transfers between devices with their start and end apart: 15, of which 8 were waited for; matrix products, arithmetic and copies ran while one was open for 0% of the time, Pallas kernels for 1%

profile of v4, /device:TPU:1, one launch (start us, length us, event | category | flops | bytes accessed | tf_op | source)
XLA Modules:
  0.0 207.2 jit_solution(5102473103207282504)
XLA Ops:
  0.7 1.2 copy-done
  1.9 0.9 copy-done.3
  2.8 0.2 shard_map.59
  3.0 5.9 %collective-permute-start = (bf16[128,1536]{1,0:T(8,128)(2,1)S(1)}, bf16[128,1536]{1,0:T(8,128)(2,1)S(1)}, u32[]{:S(2)}, u32[]{:S(2)}) collective-permute-start(bf16[128,1536]{1,0:T(8,128)(2,1)S(1)} %get-tuple-element.33), channel_id=1, source_target_pairs={{0,64},{32,96},{64,0},{96,32},{128,192},{160,224},{192,128},{224,1... | collective-permute-start | bytes 1179656 | tf_op jit(solution)/shard_map/ppermute | solution.py:17
  8.9 3.5 %collective-permute-start.2 = (bf16[128,1536]{1,0:T(8,128)(2,1)S(1)}, bf16[128,1536]{1,0:T(8,128)(2,1)S(1)}, u32[]{:S(2)}, u32[]{:S(2)}) collective-permute-start(bf16[128,1536]{1,0:T(8,128)(2,1)S(1)} %get-tuple-element.35), channel_id=1, source_target_pairs={{0,32},{32,0},{64,96},{96,64},{128,160},{160,128},{192,224},{224,1... | collective-permute-start | bytes 1179656 | tf_op jit(solution)/shard_map/ppermute | solution.py:17
  12.4 0.0 copy-start.4
  12.4 2.1 collective-permute-start.1
  14.5 8.0 %collective-permute-done.first = bf16[128,1536]{1,0:T(8,128)(2,1)S(1)} collective-permute-done((bf16[128,1536]{1,0:T(8,128)(2,1)S(1)}, bf16[128,1536]{1,0:T(8,128)(2,1)S(1)}, u32[]{:S(2)}, u32[]{:S(2)}) %collective-permute-start) | collective-permute-done | bytes 393248 | tf_op jit(solution)/shard_map/ppermute | solution.py:17
  22.5 9.7 %collective-permute-start.3 = (bf16[128,512]{1,0:T(8,128)(2,1)S(1)}, bf16[128,512]{1,0:T(8,128)(2,1)S(1)}, u32[]{:S(2)}, u32[]{:S(2)}) collective-permute-start(bf16[128,512]{1,0:T(8,128)(2,1)S(1)} %slice.97), channel_id=1, source_target_pairs={{0,32},{32,0},{64,96},{96,64},{128,160},{160,128},{192,224},{224,1... | collective-permute-start | bytes 393224 | tf_op jit(solution)/shard_map/ppermute | solution.py:17
  32.1 0.0 collective-permute-done.1.second
  32.1 0.0 collective-permute-done.2.third
  32.2 6.2 %collective-permute-done.3.relayed = bf16[128,512]{1,0:T(8,128)(2,1)S(1)} collective-permute-done((bf16[128,512]{1,0:T(8,128)(2,1)S(1)}, bf16[128,512]{1,0:T(8,128)(2,1)S(1)}, u32[]{:S(2)}, u32[]{:S(2)}) %collective-permute-start.3) | collective-permute-done | bytes 131104 | tf_op jit(solution)/shard_map/ppermute | solution.py:17
  38.4 0.8 shard_map.60
  39.2 7.5 %collective-permute-start.4 = (bf16[32,1024]{1,0:T(8,128)(2,1)S(1)}, bf16[32,1024]{1,0:T(8,128)(2,1)S(1)}, u32[]{:S(2)}, u32[]{:S(2)}) collective-permute-start(bf16[32,1024]{1,0:T(8,128)(2,1)S(1)} %get-tuple-element.47), channel_id=1, source_target_pairs={{0,128},{32,160},{64,192},{96,224},{128,256},{160,288},{192,320},{... | collective-permute-start | bytes 196616 | tf_op jit(solution)/shard_map/ppermute | solution.py:24
  46.7 10.5 %collective-permute-start.8 = (bf16[32,1024]{1,0:T(8,128)(2,1)S(1)}, bf16[32,1024]{1,0:T(8,128)(2,1)S(1)}, u32[]{:S(2)}, u32[]{:S(2)}) collective-permute-start(bf16[32,1024]{1,0:T(8,128)(2,1)S(1)} %get-tuple-element.46), channel_id=1, source_target_pairs={{0,896},{32,928},{64,960},{96,992},{128,0},{160,32},{192,64},{224,... | collective-permute-start | bytes 196616 | tf_op jit(solution)/shard_map/ppermute | solution.py:24
  57.3 0.0 copy-start.2
  57.3 0.0 collective-permute-done.4
  57.3 1.3 collective-permute-done.8
  58.6 7.4 %collective-permute-start.5 = (bf16[64,1024]{1,0:T(8,128)(2,1)S(1)}, bf16[64,1024]{1,0:T(8,128)(2,1)S(1)}, u32[]{:S(2)}, u32[]{:S(2)}) collective-permute-start(bf16[64,1024]{1,0:T(8,128)(2,1)S(1)} %get-tuple-element.45), channel_id=1, source_target_pairs={{0,128},{32,160},{64,192},{96,224},{128,256},{160,288},{192,320},{... | collective-permute-start | bytes 393224 | tf_op jit(solution)/shard_map/ppermute | solution.py:24
  66.0 2.1 %collective-permute-start.9 = (bf16[64,1024]{1,0:T(8,128)(2,1)S(1)}, bf16[64,1024]{1,0:T(8,128)(2,1)S(1)}, u32[]{:S(2)}, u32[]{:S(2)}) collective-permute-start(bf16[64,1024]{1,0:T(8,128)(2,1)S(1)} %get-tuple-element.44), channel_id=1, source_target_pairs={{0,896},{32,928},{64,960},{96,992},{128,0},{160,32},{192,64},{224,... | collective-permute-start | bytes 393224 | tf_op jit(solution)/shard_map/ppermute | solution.py:24
  68.1 0.6 collective-permute-done.5
  68.8 7.3 %collective-permute-done.9 = bf16[64,1024]{1,0:T(8,128)(2,1)S(1)} collective-permute-done((bf16[64,1024]{1,0:T(8,128)(2,1)S(1)}, bf16[64,1024]{1,0:T(8,128)(2,1)S(1)}, u32[]{:S(2)}, u32[]{:S(2)}) %collective-permute-start.9) | collective-permute-done | bytes 131104 | tf_op jit(solution)/shard_map/ppermute | solution.py:24
  76.1 0.1 fusion.1
  76.2 1.9 collective-permute-start.10
  78.1 7.3 %collective-permute-start.6 = (bf16[64,1024]{1,0:T(8,128)(2,1)S(1)}, bf16[64,1024]{1,0:T(8,128)(2,1)S(1)}, u32[]{:S(2)}, u32[]{:S(2)}) collective-permute-start(bf16[64,1024]{1,0:T(8,128)(2,1)S(1)} %get-tuple-element.43), channel_id=1, source_target_pairs={{0,128},{32,160},{64,192},{96,224},{128,256},{160,288},{192,320},{... | collective-permute-start | bytes 393224 | tf_op jit(solution)/shard_map/ppermute | solution.py:24
  85.4 4.3 %collective-permute-done.10 = bf16[64,1024]{1,0:T(8,128)(2,1)S(1)} collective-permute-done((bf16[64,1024]{1,0:T(8,128)(2,1)S(1)}, bf16[64,1024]{1,0:T(8,128)(2,1)S(1)}, u32[]{:S(2)}, u32[]{:S(2)}) %collective-permute-start.10) | collective-permute-done | bytes 131104 | tf_op jit(solution)/shard_map/ppermute | solution.py:24
  89.7 0.0 collective-permute-done.6
  89.7 0.1 fusion
  89.8 5.6 %collective-permute-start.11 = (bf16[64,1024]{1,0:T(8,128)(2,1)S(1)}, bf16[64,1024]{1,0:T(8,128)(2,1)S(1)}, u32[]{:S(2)}, u32[]{:S(2)}) collective-permute-start(bf16[64,1024]{1,0:T(8,128)(2,1)S(1)} %get-tuple-element.40), channel_id=1, source_target_pairs={{0,896},{32,928},{64,960},{96,992},{128,0},{160,32},{192,64},{224,... | collective-permute-start | bytes 393224 | tf_op jit(solution)/shard_map/ppermute | solution.py:24
  95.4 3.6 %collective-permute-start.7 = (bf16[64,1024]{1,0:T(8,128)(2,1)S(1)}, bf16[64,1024]{1,0:T(8,128)(2,1)S(1)}, u32[]{:S(2)}, u32[]{:S(2)}) collective-permute-start(bf16[64,1024]{1,0:T(8,128)(2,1)S(1)} %get-tuple-element.41), channel_id=1, source_target_pairs={{0,128},{32,160},{64,192},{96,224},{128,256},{160,288},{192,320},{... | collective-permute-start | bytes 393224 | tf_op jit(solution)/shard_map/ppermute | solution.py:24
  99.0 0.1 bitcast_convert_fusion
  99.1 12.6 %collective-permute-start.12 = (bf16[512,512]{1,0:T(8,128)(2,1)S(1)}, bf16[512,512]{1,0:T(8,128)(2,1)S(1)}, u32[]{:S(2)}, u32[]{:S(2)}) collective-permute-start(bf16[512,512]{1,0:T(8,128)(2,1)S(1)} %bitcast_convert_fusion), channel_id=1, source_target_pairs={{0,32},{32,0},{64,96},{96,64},{128,160},{160,128},{192,224},{224,1... | collective-permute-start | bytes 1572872 | tf_op jit(solution)/shard_map/ppermute | solution.py:17
  111.6 0.0 copy-start.5
  111.7 0.7 copy-done.5
  112.3 0.1 dynamic_slice.3
  112.4 0.1 select_reduce_fusion.1.chosen_ref
  112.5 0.0 collective-permute-done.11.refs_2_
  112.5 0.0 collective-permute-done.7.refs_1_
  112.5 1.5 shard_map.61
  114.0 21.7 %all-to-all-start = ((bf16[32,64,128]{2,1,0:T(8,128)(2,1)}), bf16[32,64,128]{2,1,0:T(8,128)(2,1)S(1)}, u32[]{:S(2)}, u32[]{:S(2)}) async-start(bf16[32,64,128]{2,1,0:T(8,128)(2,1)} %shard_map.61), calls=%async_computation | async-start | bytes 1048576 | tf_op jit(solution)/shard_map/all_to_all | solution.py:293
  135.8 0.2 convert_reduce_fusion
  136.0 0.1 select_reduce_fusion.source_ref
  136.1 11.3 %all-to-all-done.incoming_ref = bf16[32,64,128]{2,1,0:T(8,128)(2,1)S(1)} async-done(((bf16[32,64,128]{2,1,0:T(8,128)(2,1)}), bf16[32,64,128]{2,1,0:T(8,128)(2,1)S(1)}, u32[]{:S(2)}, u32[]{:S(2)}) %all-to-all-start) | async-done | bytes 524320 | tf_op jit(solution)/shard_map/all_to_all | solution.py:293
  147.4 0.6 shard_map.62
  148.0 37.0 %all_to_all.10.own_half = bf16[16,64,128]{2,1,0:T(8,128)(2,1)S(1)} all-to-all(bf16[16,64,128]{2,1,0:T(8,128)(2,1)S(1)} %shard_map.62), channel_id=1, replica_groups={{0,64,128,192,256,320,384,448,512,576,640,704,768,832,896,960},{32,96,1..., dimensions={0} | all-to-all | bytes 524288 | tf_op jit(solution)/shard_map/all_to_all | solution.py:295
  185.0 13.3 %collective-permute-start.13 = (bf16[16,64,128]{2,1,0:T(8,128)(2,1)S(1)}, bf16[16,64,128]{2,1,0:T(8,128)(2,1)S(1)}, u32[]{:S(2)}, u32[]{:S(2)}) collective-permute-start(bf16[16,64,128]{2,1,0:T(8,128)(2,1)S(1)} %all_to_all.10.own_half), channel_id=1, source_target_pairs={{0,32},{32,0},{64,96},{96,64},{128,160},{160,128},{192,224},{224,1... | collective-permute-start | bytes 786440 | tf_op jit(solution)/shard_map/ppermute | solution.py:17
  198.3 3.7 %collective-permute-done.13.other_half = bf16[16,64,128]{2,1,0:T(8,128)(2,1)S(1)} collective-permute-done((bf16[16,64,128]{2,1,0:T(8,128)(2,1)S(1)}, bf16[16,64,128]{2,1,0:T(8,128)(2,1)S(1)}, u32[]{:S(2)}, u32[]{:S(2)}) %collective-permute-start.13) | collective-permute-done | bytes 262176 | tf_op jit(solution)/shard_map/ppermute | solution.py:17
  202.1 5.1 %shard_map.63 = (f32[512,512]{1,0:T(8,128)}, bf16[256,512]{1,0:T(8,128)(2,1)}) custom-call(s32[1]{0:T(128)S(6)} %select_n.37.parity_ref, bf16[16,64,128]{2,1,0:T(8,128)(2,1)S(1)} %all_to_all.10.own_half, bf16[16,64,128]{2,1,0:T(8,128)(2,1)S(1)} %collective-permute-done.13.other_half, f32[512,512]{1,0:T(8,128)S(1)} %bitcast.45, ...), custom_call_target="tpu_custom_call" | custom-call | flops 2550136832 | bytes 3145728 | tf_op jit(solution)/shard_map/pallas_call | solution.py:83
  (13 shorter events, 0.1 us)
Async XLA Ops:
  0.6 1.2 copy-start
  1.9 0.9 copy-start.3
  2.8 35.6 %copy-start.1 = (bf16[128,4096]{1,0:T(8,128)(2,1)S(1)}, bf16[128,4096]{1,0:T(8,128)(2,1)}, u32[]{:S(2)}) copy-start(bf16[128,4096]{1,0:T(8,128)(2,1)} %grads_ref.3) | copy-start | bytes 3145732
  3.0 19.4 %collective-permute-start = (bf16[128,1536]{1,0:T(8,128)(2,1)S(1)}, bf16[128,1536]{1,0:T(8,128)(2,1)S(1)}, u32[]{:S(2)}, u32[]{:S(2)}) collective-permute-start(bf16[128,1536]{1,0:T(8,128)(2,1)S(1)} %get-tuple-element.33), channel_id=1, source_target_pairs={{0,64},{32,96},{64,0},{96,32},{128,192},{160,224},{192,128},{224,1... | collective-permute-start | bytes 1179656 | tf_op jit(solution)/shard_map/ppermute | solution.py:17
  8.9 23.3 %collective-permute-start.2 = (bf16[128,1536]{1,0:T(8,128)(2,1)S(1)}, bf16[128,1536]{1,0:T(8,128)(2,1)S(1)}, u32[]{:S(2)}, u32[]{:S(2)}) collective-permute-start(bf16[128,1536]{1,0:T(8,128)(2,1)S(1)} %get-tuple-element.35), channel_id=1, source_target_pairs={{0,32},{32,0},{64,96},{96,64},{128,160},{160,128},{192,224},{224,1... | collective-permute-start | bytes 1179656 | tf_op jit(solution)/shard_map/ppermute | solution.py:17
  12.4 25.9 %copy-start.4 = (bf16[128,512]{1,0:T(8,128)(2,1)S(1)}, bf16[128,512]{1,0:T(8,128)(2,1)}, u32[]{:S(2)}) copy-start(bf16[128,512]{1,0:T(8,128)(2,1)} %acts_ref.3) | copy-start | bytes 393220
  12.4 19.7 %collective-permute-start.1 = (bf16[128,1024]{1,0:T(8,128)(2,1)S(1)}, bf16[128,1024]{1,0:T(8,128)(2,1)S(1)}, u32[]{:S(2)}, u32[]{:S(2)}) collective-permute-start(bf16[128,1024]{1,0:T(8,128)(2,1)S(1)} %get-tuple-element.34), channel_id=1, source_target_pairs={{0,96},{32,64},{64,32},{96,0},{128,224},{160,192},{192,160},{224,1... | collective-permute-start | bytes 786440 | tf_op jit(solution)/shard_map/ppermute | solution.py:17
  22.5 15.9 %collective-permute-start.3 = (bf16[128,512]{1,0:T(8,128)(2,1)S(1)}, bf16[128,512]{1,0:T(8,128)(2,1)S(1)}, u32[]{:S(2)}, u32[]{:S(2)}) collective-permute-start(bf16[128,512]{1,0:T(8,128)(2,1)S(1)} %slice.97), channel_id=1, source_target_pairs={{0,32},{32,0},{64,96},{96,64},{128,160},{160,128},{192,224},{224,1... | collective-permute-start | bytes 393224 | tf_op jit(solution)/shard_map/ppermute | solution.py:17
  39.2 18.1 %collective-permute-start.4 = (bf16[32,1024]{1,0:T(8,128)(2,1)S(1)}, bf16[32,1024]{1,0:T(8,128)(2,1)S(1)}, u32[]{:S(2)}, u32[]{:S(2)}) collective-permute-start(bf16[32,1024]{1,0:T(8,128)(2,1)S(1)} %get-tuple-element.47), channel_id=1, source_target_pairs={{0,128},{32,160},{64,192},{96,224},{128,256},{160,288},{192,320},{... | collective-permute-start | bytes 196616 | tf_op jit(solution)/shard_map/ppermute | solution.py:24
  46.7 11.9 %collective-permute-start.8 = (bf16[32,1024]{1,0:T(8,128)(2,1)S(1)}, bf16[32,1024]{1,0:T(8,128)(2,1)S(1)}, u32[]{:S(2)}, u32[]{:S(2)}) collective-permute-start(bf16[32,1024]{1,0:T(8,128)(2,1)S(1)} %get-tuple-element.46), channel_id=1, source_target_pairs={{0,896},{32,928},{64,960},{96,992},{128,0},{160,32},{192,64},{224,... | collective-permute-start | bytes 196616 | tf_op jit(solution)/shard_map/ppermute | solution.py:24
  57.3 41.7 %copy-start.2 = (f32[1,1,512,512]{3,2,1,0:T(8,128)S(1)}, f32[1,1,512,512]{3,2,1,0:T(8,128)}, u32[]{:S(2)}) copy-start(f32[1,1,512,512]{3,2,1,0:T(8,128)} %param.11) | copy-start | bytes 3145732
  58.6 10.2 %collective-permute-start.5 = (bf16[64,1024]{1,0:T(8,128)(2,1)S(1)}, bf16[64,1024]{1,0:T(8,128)(2,1)S(1)}, u32[]{:S(2)}, u32[]{:S(2)}) collective-permute-start(bf16[64,1024]{1,0:T(8,128)(2,1)S(1)} %get-tuple-element.45), channel_id=1, source_target_pairs={{0,128},{32,160},{64,192},{96,224},{128,256},{160,288},{192,320},{... | collective-permute-start | bytes 393224 | tf_op jit(solution)/shard_map/ppermute | solution.py:24
  66.0 10.1 %collective-permute-start.9 = (bf16[64,1024]{1,0:T(8,128)(2,1)S(1)}, bf16[64,1024]{1,0:T(8,128)(2,1)S(1)}, u32[]{:S(2)}, u32[]{:S(2)}) collective-permute-start(bf16[64,1024]{1,0:T(8,128)(2,1)S(1)} %get-tuple-element.44), channel_id=1, source_target_pairs={{0,896},{32,928},{64,960},{96,992},{128,0},{160,32},{192,64},{224,... | collective-permute-start | bytes 393224 | tf_op jit(solution)/shard_map/ppermute | solution.py:24
  76.2 13.5 %collective-permute-start.10 = (bf16[64,1024]{1,0:T(8,128)(2,1)S(1)}, bf16[64,1024]{1,0:T(8,128)(2,1)S(1)}, u32[]{:S(2)}, u32[]{:S(2)}) collective-permute-start(bf16[64,1024]{1,0:T(8,128)(2,1)S(1)} %get-tuple-element.42), channel_id=1, source_target_pairs={{0,896},{32,928},{64,960},{96,992},{128,0},{160,32},{192,64},{224,... | collective-permute-start | bytes 393224 | tf_op jit(solution)/shard_map/ppermute | solution.py:24
  78.1 11.6 %collective-permute-start.6 = (bf16[64,1024]{1,0:T(8,128)(2,1)S(1)}, bf16[64,1024]{1,0:T(8,128)(2,1)S(1)}, u32[]{:S(2)}, u32[]{:S(2)}) collective-permute-start(bf16[64,1024]{1,0:T(8,128)(2,1)S(1)} %get-tuple-element.43), channel_id=1, source_target_pairs={{0,128},{32,160},{64,192},{96,224},{128,256},{160,288},{192,320},{... | collective-permute-start | bytes 393224 | tf_op jit(solution)/shard_map/ppermute | solution.py:24
  89.8 22.7 %collective-permute-start.11 = (bf16[64,1024]{1,0:T(8,128)(2,1)S(1)}, bf16[64,1024]{1,0:T(8,128)(2,1)S(1)}, u32[]{:S(2)}, u32[]{:S(2)}) collective-permute-start(bf16[64,1024]{1,0:T(8,128)(2,1)S(1)} %get-tuple-element.40), channel_id=1, source_target_pairs={{0,896},{32,928},{64,960},{96,992},{128,0},{160,32},{192,64},{224,... | collective-permute-start | bytes 393224 | tf_op jit(solution)/shard_map/ppermute | solution.py:24
  95.4 17.1 %collective-permute-start.7 = (bf16[64,1024]{1,0:T(8,128)(2,1)S(1)}, bf16[64,1024]{1,0:T(8,128)(2,1)S(1)}, u32[]{:S(2)}, u32[]{:S(2)}) collective-permute-start(bf16[64,1024]{1,0:T(8,128)(2,1)S(1)} %get-tuple-element.41), channel_id=1, source_target_pairs={{0,128},{32,160},{64,192},{96,224},{128,256},{160,288},{192,320},{... | collective-permute-start | bytes 393224 | tf_op jit(solution)/shard_map/ppermute | solution.py:24
  99.1 37.1 %collective-permute-start.12 = (bf16[512,512]{1,0:T(8,128)(2,1)S(1)}, bf16[512,512]{1,0:T(8,128)(2,1)S(1)}, u32[]{:S(2)}, u32[]{:S(2)}) collective-permute-start(bf16[512,512]{1,0:T(8,128)(2,1)S(1)} %bitcast_convert_fusion), channel_id=1, source_target_pairs={{0,32},{32,0},{64,96},{96,64},{128,160},{160,128},{192,224},{224,1... | collective-permute-start | bytes 1572872 | tf_op jit(solution)/shard_map/ppermute | solution.py:17
  111.6 0.7 copy-start.5
  114.0 33.4 %all-to-all-start = ((bf16[32,64,128]{2,1,0:T(8,128)(2,1)}), bf16[32,64,128]{2,1,0:T(8,128)(2,1)S(1)}, u32[]{:S(2)}, u32[]{:S(2)}) async-start(bf16[32,64,128]{2,1,0:T(8,128)(2,1)} %shard_map.61), calls=%async_computation | async-start | bytes 1048576 | tf_op jit(solution)/shard_map/all_to_all | solution.py:293
  185.0 17.1 %collective-permute-start.13 = (bf16[16,64,128]{2,1,0:T(8,128)(2,1)S(1)}, bf16[16,64,128]{2,1,0:T(8,128)(2,1)S(1)}, u32[]{:S(2)}, u32[]{:S(2)}) collective-permute-start(bf16[16,64,128]{2,1,0:T(8,128)(2,1)S(1)} %all_to_all.10.own_half), channel_id=1, source_target_pairs={{0,32},{32,0},{64,96},{96,64},{128,160},{160,128},{192,224},{224,1... | collective-permute-start | bytes 786440 | tf_op jit(solution)/shard_map/ppermute | solution.py:17

commit v5 on v4

--- a/solution.py
+++ b/solution.py
@@ -284,10 +284,14 @@
     source = jnp.max(jnp.where(placing, block_ids[None, :] // per_group, -1), axis=1)
 
     own_factor = factors[0, 0]
-    other_factor = across(own_factor.astype(jnp.bfloat16), 1)
+    factor_low = own_factor.astype(jnp.bfloat16)
     sent = team_messages(member, acts, grads_out)
     messages = [across(message, mask) for mask, message in zip((2, 3, 1), sent)]
     messages.append(across(messages[0][:, :block_width], 1))
+    *messages, chosen, source, factor_low = lax.optimization_barrier(
+        (*messages, chosen, source, factor_low)
+    )
+    other_factor = across(factor_low, 1)
     terms = ring_terms(team_gradient(member, place, stops, acts, grads_out, messages))
     outgoing = by_owner(chosen, terms, block_width // team)
     incoming = lax.all_to_all(outgoing, "grp", split_axis=0, concat_axis=0, tiled=True)

time: 211 us -> 217 us (1.028)
  starting transfers between devices: 115 us -> 94.2 us
  waiting for transfers between devices: 42.7 us -> 62.4 us
  blocking collectives: 37 us -> 44.8 us
    ppermute x6, starting transfers between devices: 47 us -> 19.7 us  [across(): lax.ppermute(block, 'dp', [(place, place ^ mask) for place in range(lax.a...]
    ppermute x6, waiting for transfers between devices: 17.9 us -> 30 us  [across(): lax.ppermute(block, 'dp', [(place, place ^ mask) for place in range(lax.a...]
    all_to_all x1, blocking collectives: 37 us -> 44.8 us  [per_device(): lax.all_to_all(by_slot(source, incoming), 'dp', split_axis=0, concat_axis...]
    ppermute x8, waiting for transfers between devices: 13.6 us -> 20.7 us  [along(): lax.ppermute(block, 'dp', [(place, (place + distance) % count) for place...]
    all_to_all x1, starting transfers between devices: 21.7 us -> 25.8 us  [per_device(): lax.all_to_all(outgoing, 'grp', split_axis=0, concat_axis=0, tiled=True)]
    ppermute x8, starting transfers between devices: 45.9 us -> 48.6 us  [along(): lax.ppermute(block, 'dp', [(place, (place + distance) % count) for place...]
  transfers between devices with their start and end apart: 15 -> 15, of which waited for: 8 -> 11; matrix products, arithmetic and copies ran while one was open for 0% -> 1% of each run, Pallas kernels for 1% -> 1%
where the time goes in v5:
time: 217 us; the launch traced here: 215 us
  starting transfers between devices  94.2 us (43%)
  waiting for transfers between devices  62.4 us (29%)
  blocking collectives  44.8 us (21%)
  Pallas kernels  9.26 us (4%)
  local copies, waits for them, and re-layouts  2.27 us (1%)
    ppermute x8, starting transfers between devices, along(): lax.ppermute(block, 'dp', [(place, (place + distance) % count) for place...  48.6 us
    all_to_all x1, blocking collectives, per_device(): lax.all_to_all(by_slot(source, incoming), 'dp', split_axis=0, concat_axis...  44.8 us
    ppermute x6, waiting for transfers between devices, across(): lax.ppermute(block, 'dp', [(place, place ^ mask) for place in range(lax.a...  30 us
    all_to_all x1, starting transfers between devices, per_device(): lax.all_to_all(outgoing, 'grp', split_axis=0, concat_axis=0, tiled=True)  25.8 us
    ppermute x8, waiting for transfers between devices, along(): lax.ppermute(block, 'dp', [(place, (place + distance) % count) for place...  20.7 us
    ppermute x6, starting transfers between devices, across(): lax.ppermute(block, 'dp', [(place, place ^ mask) for place in range(lax.a...  19.7 us
    all_to_all x1, waiting for transfers between devices, per_device(): lax.all_to_all(outgoing, 'grp', split_axis=0, concat_axis=0, tiled=True)  11.6 us
    pallas_call x1, Pallas kernels, precondition(): pl.pallas_call(precondition_kernel, out_shape=(jax.ShapeDtypeStruct((size...  5.1 us
  transfers between devices with their start and end apart: 15, of which 11 were waited for; matrix products, arithmetic and copies ran while one was open for 1% of the time, Pallas kernels for 1%

profile of v5, /device:TPU:1, one launch (start us, length us, event | category | flops | bytes accessed | tf_op | source)
XLA Modules:
  0.0 215.3 jit_solution(3789788700206740501)
XLA Ops:
  0.6 0.0 copy-start
  0.7 1.2 copy-done
  1.9 0.9 copy-done.3
  2.8 1.2 shard_map.59
  4.0 7.2 %collective-permute-start.1 = (bf16[128,1024]{1,0:T(8,128)(2,1)}, bf16[128,1024]{1,0:T(8,128)(2,1)S(1)}, u32[]{:S(2)}, u32[]{:S(2)}) collective-permute-start(bf16[128,1024]{1,0:T(8,128)(2,1)} %get-tuple-element.41), channel_id=1, source_target_pairs={{0,96},{32,64},{64,32},{96,0},{128,224},{160,192},{192,160},{224,1... | collective-permute-start | bytes 786440 | tf_op jit(solution)/shard_map/ppermute | solution.py:17
  11.2 1.9 collective-permute-start
  13.1 2.2 %collective-permute-start.2 = (bf16[128,1536]{1,0:T(8,128)(2,1)}, bf16[128,1536]{1,0:T(8,128)(2,1)S(1)}, u32[]{:S(2)}, u32[]{:S(2)}) collective-permute-start(bf16[128,1536]{1,0:T(8,128)(2,1)} %get-tuple-element.42), channel_id=1, source_target_pairs={{0,32},{32,0},{64,96},{96,64},{128,160},{160,128},{192,224},{224,1... | collective-permute-start | bytes 1179656 | tf_op jit(solution)/shard_map/ppermute | solution.py:17
  15.3 0.0 copy-start.6
  15.3 0.9 bitcast_convert_fusion
  16.2 0.2 convert_reduce_fusion
  16.4 0.0 copy-start.4
  16.4 21.4 %collective-permute-done.first = bf16[128,1536]{1,0:T(8,128)(2,1)S(1)} collective-permute-done((bf16[128,1536]{1,0:T(8,128)(2,1)}, bf16[128,1536]{1,0:T(8,128)(2,1)S(1)}, u32[]{:S(2)}, u32[]{:S(2)}) %collective-permute-start) | collective-permute-done | bytes 393248 | tf_op jit(solution)/shard_map/ppermute | solution.py:17
  37.8 2.0 collective-permute-start.3
  39.8 0.1 select_reduce_fusion.source_ref
  40.0 0.1 dynamic_slice.3
  40.0 0.1 select_reduce_fusion.1.chosen_ref
  40.1 0.0 collective-permute-done.1.second
  40.1 0.0 collective-permute-done.2.third
  40.1 3.4 %collective-permute-done.3.relayed = bf16[128,512]{1,0:T(8,128)(2,1)S(1)} collective-permute-done((bf16[128,512]{1,0:T(8,128)(2,1)S(1)}, bf16[128,512]{1,0:T(8,128)(2,1)S(1)}, u32[]{:S(2)}, u32[]{:S(2)}) %collective-permute-start.3) | collective-permute-done | bytes 131104 | tf_op jit(solution)/shard_map/ppermute | solution.py:17
  43.6 0.8 shard_map.60
  44.4 19.0 %collective-permute-start.8 = (bf16[32,1024]{1,0:T(8,128)(2,1)S(1)}, bf16[32,1024]{1,0:T(8,128)(2,1)S(1)}, u32[]{:S(2)}, u32[]{:S(2)}) collective-permute-start(bf16[32,1024]{1,0:T(8,128)(2,1)S(1)} %get-tuple-element.60), channel_id=1, source_target_pairs={{0,896},{32,928},{64,960},{96,992},{128,0},{160,32},{192,64},{224,... | collective-permute-start | bytes 196616 | tf_op jit(solution)/shard_map/ppermute | solution.py:24
  63.4 1.9 collective-permute-start.4
  65.4 1.1 collective-permute-done.8
  66.5 5.9 %collective-permute-done.4 = bf16[32,1024]{1,0:T(8,128)(2,1)S(1)} collective-permute-done((bf16[32,1024]{1,0:T(8,128)(2,1)S(1)}, bf16[32,1024]{1,0:T(8,128)(2,1)S(1)}, u32[]{:S(2)}, u32[]{:S(2)}) %collective-permute-start.4) | collective-permute-done | bytes 65568 | tf_op jit(solution)/shard_map/ppermute | solution.py:24
  72.4 5.2 %collective-permute-start.9 = (bf16[64,1024]{1,0:T(8,128)(2,1)S(1)}, bf16[64,1024]{1,0:T(8,128)(2,1)S(1)}, u32[]{:S(2)}, u32[]{:S(2)}) collective-permute-start(bf16[64,1024]{1,0:T(8,128)(2,1)S(1)} %get-tuple-element.58), channel_id=1, source_target_pairs={{0,896},{32,928},{64,960},{96,992},{128,0},{160,32},{192,64},{224,... | collective-permute-start | bytes 393224 | tf_op jit(solution)/shard_map/ppermute | solution.py:24
  77.6 4.0 %collective-permute-start.5 = (bf16[64,1024]{1,0:T(8,128)(2,1)S(1)}, bf16[64,1024]{1,0:T(8,128)(2,1)S(1)}, u32[]{:S(2)}, u32[]{:S(2)}) collective-permute-start(bf16[64,1024]{1,0:T(8,128)(2,1)S(1)} %get-tuple-element.59), channel_id=1, source_target_pairs={{0,128},{32,160},{64,192},{96,224},{128,256},{160,288},{192,320},{... | collective-permute-start | bytes 393224 | tf_op jit(solution)/shard_map/ppermute | solution.py:24
  81.6 5.8 %collective-permute-done.9 = bf16[64,1024]{1,0:T(8,128)(2,1)S(1)} collective-permute-done((bf16[64,1024]{1,0:T(8,128)(2,1)S(1)}, bf16[64,1024]{1,0:T(8,128)(2,1)S(1)}, u32[]{:S(2)}, u32[]{:S(2)}) %collective-permute-start.9) | collective-permute-done | bytes 131104 | tf_op jit(solution)/shard_map/ppermute | solution.py:24
  87.4 0.1 collective-permute-done.5
  87.5 0.1 fusion.1
  87.6 0.0 copy-start.5
  87.6 5.3 %collective-permute-start.10 = (bf16[64,1024]{1,0:T(8,128)(2,1)S(1)}, bf16[64,1024]{1,0:T(8,128)(2,1)S(1)}, u32[]{:S(2)}, u32[]{:S(2)}) collective-permute-start(bf16[64,1024]{1,0:T(8,128)(2,1)S(1)} %get-tuple-element.56), channel_id=1, source_target_pairs={{0,896},{32,928},{64,960},{96,992},{128,0},{160,32},{192,64},{224,... | collective-permute-start | bytes 393224 | tf_op jit(solution)/shard_map/ppermute | solution.py:24
  92.9 4.0 %collective-permute-start.6 = (bf16[64,1024]{1,0:T(8,128)(2,1)S(1)}, bf16[64,1024]{1,0:T(8,128)(2,1)S(1)}, u32[]{:S(2)}, u32[]{:S(2)}) collective-permute-start(bf16[64,1024]{1,0:T(8,128)(2,1)S(1)} %get-tuple-element.57), channel_id=1, source_target_pairs={{0,128},{32,160},{64,192},{96,224},{128,256},{160,288},{192,320},{... | collective-permute-start | bytes 393224 | tf_op jit(solution)/shard_map/ppermute | solution.py:24
  96.9 0.7 collective-permute-done.10
  97.6 5.2 %collective-permute-done.6 = bf16[64,1024]{1,0:T(8,128)(2,1)S(1)} collective-permute-done((bf16[64,1024]{1,0:T(8,128)(2,1)S(1)}, bf16[64,1024]{1,0:T(8,128)(2,1)S(1)}, u32[]{:S(2)}, u32[]{:S(2)}) %collective-permute-start.6) | collective-permute-done | bytes 131104 | tf_op jit(solution)/shard_map/ppermute | solution.py:24
  102.8 0.1 fusion
  102.9 6.0 %collective-permute-start.11 = (bf16[64,1024]{1,0:T(8,128)(2,1)S(1)}, bf16[64,1024]{1,0:T(8,128)(2,1)S(1)}, u32[]{:S(2)}, u32[]{:S(2)}) collective-permute-start(bf16[64,1024]{1,0:T(8,128)(2,1)S(1)} %get-tuple-element.54), channel_id=1, source_target_pairs={{0,896},{32,928},{64,960},{96,992},{128,0},{160,32},{192,64},{224,... | collective-permute-start | bytes 393224 | tf_op jit(solution)/shard_map/ppermute | solution.py:24
  108.9 3.2 %collective-permute-start.7 = (bf16[64,1024]{1,0:T(8,128)(2,1)S(1)}, bf16[64,1024]{1,0:T(8,128)(2,1)S(1)}, u32[]{:S(2)}, u32[]{:S(2)}) collective-permute-start(bf16[64,1024]{1,0:T(8,128)(2,1)S(1)} %get-tuple-element.55), channel_id=1, source_target_pairs={{0,128},{32,160},{64,192},{96,224},{128,256},{160,288},{192,320},{... | collective-permute-start | bytes 393224 | tf_op jit(solution)/shard_map/ppermute | solution.py:24
  112.1 4.5 %collective-permute-start.12 = (bf16[512,512]{1,0:T(8,128)(2,1)S(1)}, bf16[512,512]{1,0:T(8,128)(2,1)S(1)}, u32[]{:S(2)}, u32[]{:S(2)}) collective-permute-start(bf16[512,512]{1,0:T(8,128)(2,1)S(1)} %copy-done.5), channel_id=1, source_target_pairs={{0,32},{32,0},{64,96},{96,64},{128,160},{160,128},{192,224},{224,1... | collective-permute-start | bytes 1572872 | tf_op jit(solution)/shard_map/ppermute | solution.py:17
  116.6 0.0 collective-permute-done.11.refs_2_
  116.6 2.0 collective-permute-done.7.refs_1_
  118.6 1.5 shard_map.61
  120.2 25.8 %all-to-all-start = ((bf16[32,64,128]{2,1,0:T(8,128)(2,1)}), bf16[32,64,128]{2,1,0:T(8,128)(2,1)S(1)}, u32[]{:S(2)}, u32[]{:S(2)}) async-start(bf16[32,64,128]{2,1,0:T(8,128)(2,1)} %shard_map.61), calls=%async_computation | async-start | bytes 1048576 | tf_op jit(solution)/shard_map/all_to_all | solution.py:297
  146.0 11.6 %all-to-all-done.incoming_ref = bf16[32,64,128]{2,1,0:T(8,128)(2,1)S(1)} async-done(((bf16[32,64,128]{2,1,0:T(8,128)(2,1)}), bf16[32,64,128]{2,1,0:T(8,128)(2,1)S(1)}, u32[]{:S(2)}, u32[]{:S(2)}) %all-to-all-start) | async-done | bytes 524320 | tf_op jit(solution)/shard_map/all_to_all | solution.py:297
  157.6 0.6 shard_map.62
  158.2 44.8 %all_to_all.10.own_half = bf16[16,64,128]{2,1,0:T(8,128)(2,1)S(1)} all-to-all(bf16[16,64,128]{2,1,0:T(8,128)(2,1)S(1)} %shard_map.62), channel_id=1, replica_groups={{0,64,128,192,256,320,384,448,512,576,640,704,768,832,896,960},{32,96,1..., dimensions={0} | all-to-all | bytes 524288 | tf_op jit(solution)/shard_map/all_to_all | solution.py:299
  203.1 1.9 collective-permute-start.13
  205.0 5.2 %collective-permute-done.13.other_half = bf16[16,64,128]{2,1,0:T(8,128)(2,1)S(1)} collective-permute-done((bf16[16,64,128]{2,1,0:T(8,128)(2,1)S(1)}, bf16[16,64,128]{2,1,0:T(8,128)(2,1)S(1)}, u32[]{:S(2)}, u32[]{:S(2)}) %collective-permute-start.13) | collective-permute-done | bytes 262176 | tf_op jit(solution)/shard_map/ppermute | solution.py:17
  210.2 5.1 %shard_map.63 = (f32[512,512]{1,0:T(8,128)}, bf16[256,512]{1,0:T(8,128)(2,1)}) custom-call(s32[1]{0:T(128)S(6)} %select_n.37.parity_ref, bf16[16,64,128]{2,1,0:T(8,128)(2,1)S(1)} %all_to_all.10.own_half, bf16[16,64,128]{2,1,0:T(8,128)(2,1)S(1)} %collective-permute-done.13.other_half, f32[512,512]{1,0:T(8,128)S(1)} %bitcast.45, ...), custom_call_target="tpu_custom_call" | custom-call | flops 2550136832 | bytes 3145728 | tf_op jit(solution)/shard_map/pallas_call | solution.py:83
  (15 shorter events, 0.1 us)
Async XLA Ops:
  0.6 1.2 copy-start
  1.9 0.9 copy-start.3
  2.8 12.5 %copy-start.2 = (f32[1,1,512,512]{3,2,1,0:T(8,128)S(1)}, f32[1,1,512,512]{3,2,1,0:T(8,128)}, u32[]{:S(2)}) copy-start(f32[1,1,512,512]{3,2,1,0:T(8,128)} %param.11) | copy-start | bytes 3145732
  4.0 39.6 %copy-start.1 = (bf16[128,4096]{1,0:T(8,128)(2,1)S(1)}, bf16[128,4096]{1,0:T(8,128)(2,1)}, u32[]{:S(2)}) copy-start(bf16[128,4096]{1,0:T(8,128)(2,1)} %grads_ref.3) | copy-start | bytes 3145732
  4.0 36.2 %collective-permute-start.1 = (bf16[128,1024]{1,0:T(8,128)(2,1)}, bf16[128,1024]{1,0:T(8,128)(2,1)S(1)}, u32[]{:S(2)}, u32[]{:S(2)}) collective-permute-start(bf16[128,1024]{1,0:T(8,128)(2,1)} %get-tuple-element.41), channel_id=1, source_target_pairs={{0,96},{32,64},{64,32},{96,0},{128,224},{160,192},{192,160},{224,1... | collective-permute-start | bytes 786440 | tf_op jit(solution)/shard_map/ppermute | solution.py:17
  11.2 26.6 %collective-permute-start = (bf16[128,1536]{1,0:T(8,128)(2,1)}, bf16[128,1536]{1,0:T(8,128)(2,1)S(1)}, u32[]{:S(2)}, u32[]{:S(2)}) collective-permute-start(bf16[128,1536]{1,0:T(8,128)(2,1)} %get-tuple-element.40), channel_id=1, source_target_pairs={{0,64},{32,96},{64,0},{96,32},{128,192},{160,224},{192,128},{224,1... | collective-permute-start | bytes 1179656 | tf_op jit(solution)/shard_map/ppermute | solution.py:17
  13.1 27.0 %collective-permute-start.2 = (bf16[128,1536]{1,0:T(8,128)(2,1)}, bf16[128,1536]{1,0:T(8,128)(2,1)S(1)}, u32[]{:S(2)}, u32[]{:S(2)}) collective-permute-start(bf16[128,1536]{1,0:T(8,128)(2,1)} %get-tuple-element.42), channel_id=1, source_target_pairs={{0,32},{32,0},{64,96},{96,64},{128,160},{160,128},{192,224},{224,1... | collective-permute-start | bytes 1179656 | tf_op jit(solution)/shard_map/ppermute | solution.py:17
  15.3 0.9 copy-start.6
  16.4 27.2 %copy-start.4 = (bf16[128,512]{1,0:T(8,128)(2,1)S(1)}, bf16[128,512]{1,0:T(8,128)(2,1)}, u32[]{:S(2)}) copy-start(bf16[128,512]{1,0:T(8,128)(2,1)} %acts_ref.3) | copy-start | bytes 393220
  37.8 5.7 %collective-permute-start.3 = (bf16[128,512]{1,0:T(8,128)(2,1)S(1)}, bf16[128,512]{1,0:T(8,128)(2,1)S(1)}, u32[]{:S(2)}, u32[]{:S(2)}) collective-permute-start(bf16[128,512]{1,0:T(8,128)(2,1)S(1)} %slice.97), channel_id=1, source_target_pairs={{0,32},{32,0},{64,96},{96,64},{128,160},{160,128},{192,224},{224,1... | collective-permute-start | bytes 393224 | tf_op jit(solution)/shard_map/ppermute | solution.py:17
  44.4 22.1 %collective-permute-start.8 = (bf16[32,1024]{1,0:T(8,128)(2,1)S(1)}, bf16[32,1024]{1,0:T(8,128)(2,1)S(1)}, u32[]{:S(2)}, u32[]{:S(2)}) collective-permute-start(bf16[32,1024]{1,0:T(8,128)(2,1)S(1)} %get-tuple-element.60), channel_id=1, source_target_pairs={{0,896},{32,928},{64,960},{96,992},{128,0},{160,32},{192,64},{224,... | collective-permute-start | bytes 196616 | tf_op jit(solution)/shard_map/ppermute | solution.py:24
  63.4 8.9 %collective-permute-start.4 = (bf16[32,1024]{1,0:T(8,128)(2,1)S(1)}, bf16[32,1024]{1,0:T(8,128)(2,1)S(1)}, u32[]{:S(2)}, u32[]{:S(2)}) collective-permute-start(bf16[32,1024]{1,0:T(8,128)(2,1)S(1)} %get-tuple-element.61), channel_id=1, source_target_pairs={{0,128},{32,160},{64,192},{96,224},{128,256},{160,288},{192,320},{... | collective-permute-start | bytes 196616 | tf_op jit(solution)/shard_map/ppermute | solution.py:24
  72.4 15.0 %collective-permute-start.9 = (bf16[64,1024]{1,0:T(8,128)(2,1)S(1)}, bf16[64,1024]{1,0:T(8,128)(2,1)S(1)}, u32[]{:S(2)}, u32[]{:S(2)}) collective-permute-start(bf16[64,1024]{1,0:T(8,128)(2,1)S(1)} %get-tuple-element.58), channel_id=1, source_target_pairs={{0,896},{32,928},{64,960},{96,992},{128,0},{160,32},{192,64},{224,... | collective-permute-start | bytes 393224 | tf_op jit(solution)/shard_map/ppermute | solution.py:24
  77.6 9.9 %collective-permute-start.5 = (bf16[64,1024]{1,0:T(8,128)(2,1)S(1)}, bf16[64,1024]{1,0:T(8,128)(2,1)S(1)}, u32[]{:S(2)}, u32[]{:S(2)}) collective-permute-start(bf16[64,1024]{1,0:T(8,128)(2,1)S(1)} %get-tuple-element.59), channel_id=1, source_target_pairs={{0,128},{32,160},{64,192},{96,224},{128,256},{160,288},{192,320},{... | collective-permute-start | bytes 393224 | tf_op jit(solution)/shard_map/ppermute | solution.py:24
  87.6 24.5 %copy-start.5 = (bf16[512,512]{1,0:T(8,128)(2,1)S(1)}, bf16[512,512]{1,0:T(8,128)(2,1)}, u32[]{:S(2)}) copy-start(bf16[512,512]{1,0:T(8,128)(2,1)} %bitcast_convert_fusion) | copy-start | bytes 1572868
  87.6 10.1 %collective-permute-start.10 = (bf16[64,1024]{1,0:T(8,128)(2,1)S(1)}, bf16[64,1024]{1,0:T(8,128)(2,1)S(1)}, u32[]{:S(2)}, u32[]{:S(2)}) collective-permute-start(bf16[64,1024]{1,0:T(8,128)(2,1)S(1)} %get-tuple-element.56), channel_id=1, source_target_pairs={{0,896},{32,928},{64,960},{96,992},{128,0},{160,32},{192,64},{224,... | collective-permute-start | bytes 393224 | tf_op jit(solution)/shard_map/ppermute | solution.py:24
  92.9 9.9 %collective-permute-start.6 = (bf16[64,1024]{1,0:T(8,128)(2,1)S(1)}, bf16[64,1024]{1,0:T(8,128)(2,1)S(1)}, u32[]{:S(2)}, u32[]{:S(2)}) collective-permute-start(bf16[64,1024]{1,0:T(8,128)(2,1)S(1)} %get-tuple-element.57), channel_id=1, source_target_pairs={{0,128},{32,160},{64,192},{96,224},{128,256},{160,288},{192,320},{... | collective-permute-start | bytes 393224 | tf_op jit(solution)/shard_map/ppermute | solution.py:24
  102.9 13.7 %collective-permute-start.11 = (bf16[64,1024]{1,0:T(8,128)(2,1)S(1)}, bf16[64,1024]{1,0:T(8,128)(2,1)S(1)}, u32[]{:S(2)}, u32[]{:S(2)}) collective-permute-start(bf16[64,1024]{1,0:T(8,128)(2,1)S(1)} %get-tuple-element.54), channel_id=1, source_target_pairs={{0,896},{32,928},{64,960},{96,992},{128,0},{160,32},{192,64},{224,... | collective-permute-start | bytes 393224 | tf_op jit(solution)/shard_map/ppermute | solution.py:24
  108.9 9.7 %collective-permute-start.7 = (bf16[64,1024]{1,0:T(8,128)(2,1)S(1)}, bf16[64,1024]{1,0:T(8,128)(2,1)S(1)}, u32[]{:S(2)}, u32[]{:S(2)}) collective-permute-start(bf16[64,1024]{1,0:T(8,128)(2,1)S(1)} %get-tuple-element.55), channel_id=1, source_target_pairs={{0,128},{32,160},{64,192},{96,224},{128,256},{160,288},{192,320},{... | collective-permute-start | bytes 393224 | tf_op jit(solution)/shard_map/ppermute | solution.py:24
  112.1 33.9 %collective-permute-start.12 = (bf16[512,512]{1,0:T(8,128)(2,1)S(1)}, bf16[512,512]{1,0:T(8,128)(2,1)S(1)}, u32[]{:S(2)}, u32[]{:S(2)}) collective-permute-start(bf16[512,512]{1,0:T(8,128)(2,1)S(1)} %copy-done.5), channel_id=1, source_target_pairs={{0,32},{32,0},{64,96},{96,64},{128,160},{160,128},{192,224},{224,1... | collective-permute-start | bytes 1572872 | tf_op jit(solution)/shard_map/ppermute | solution.py:17
  120.2 37.4 %all-to-all-start = ((bf16[32,64,128]{2,1,0:T(8,128)(2,1)}), bf16[32,64,128]{2,1,0:T(8,128)(2,1)S(1)}, u32[]{:S(2)}, u32[]{:S(2)}) async-start(bf16[32,64,128]{2,1,0:T(8,128)(2,1)} %shard_map.61), calls=%async_computation | async-start | bytes 1048576 | tf_op jit(solution)/shard_map/all_to_all | solution.py:297
  203.1 7.1 %collective-permute-start.13 = (bf16[16,64,128]{2,1,0:T(8,128)(2,1)S(1)}, bf16[16,64,128]{2,1,0:T(8,128)(2,1)S(1)}, u32[]{:S(2)}, u32[]{:S(2)}) collective-permute-start(bf16[16,64,128]{2,1,0:T(8,128)(2,1)S(1)} %all_to_all.10.own_half), channel_id=1, source_target_pairs={{0,32},{32,0},{64,96},{96,64},{128,160},{160,128},{192,224},{224,1... | collective-permute-start | bytes 786440 | tf_op jit(solution)/shard_map/ppermute | solution.py:17
